TPU v7x, 32 devices: a whole 2x2x4 slice. The times are simulated.
32 devices in a mesh: level: 2 (over x), row: 4 (over y, core), col: 4 (over z).
Axes of the slice: x: 2, y: 2, z: 4, core: 2. Of those that a mesh axis runs over, the one named last changes fastest.
Arguments:
- initials: float32 [4096, 4, 1536], P(('level', 'row'), 'col'), may hold values from -70 to 70, as said below
- patches: int32 [2, 32], replicated, may hold values from 0 to 5
- halves: int32 [1, 32], replicated, may hold values 0 or 1
Outputs:
- panels: float32 [2, 4096, 512], P(None, ('level', 'row'), 'col')
- root_update: float32 [4096, 4, 1024], P(('level', 'row'), 'col')
Inputs may be any that keep to these rules, and one draw needn't show every extreme that they name: Each front's block of initials is symmetric, and stays positive definite when multiplied by the tile mask of its level's patches.
All inputs are finite; a program needn't handle non-finite values.
Results may differ from a plain program's by a relative error of at most 0.0001.
Values sent between devices are 32-bit elements; how exact they have to be, the bound alone decides.
A program may use at most 192 MiB of HBM per device.

v0:
```python
import jax
import jax.numpy as jnp
from jax import lax
from jax.sharding import PartitionSpec as P


def from_partner(value, axis, bit):
    mask = 2**bit
    pairs = [(source, source ^ mask) for source in range(lax.axis_size(axis))]
    return lax.ppermute(value, axis, pairs)


def pick_column(vector, start, count_j, n_col, col_idx):
    segment = lax.dynamic_slice_in_dim(vector, start, count_j * n_col).reshape(count_j, n_col)
    onehot = jnp.arange(n_col) == col_idx
    return jnp.sum(jnp.where(onehot[None, :], segment, 0), axis=1)


def place_update(update, row_half, col_half, side, tile):
    row_keep = jnp.repeat((row_half == side).astype(jnp.float32), tile)
    col_high = jnp.repeat(col_half.astype(jnp.float32), tile)
    lower_part = update * (1.0 - col_high)[None, :]
    upper_part = update * col_high[None, :]
    return row_keep[:, None] * jnp.concatenate([lower_part, upper_part], axis=1)


def local(initials, patches, halves):
    n_level = lax.axis_size("level")
    n_row = lax.axis_size("row")
    n_col = lax.axis_size("col")
    levels = n_level.bit_length()
    lvl = lax.axis_index("level")
    row_idx = lax.axis_index("row")
    col_idx = lax.axis_index("col")
    rows_dev = initials.shape[0]
    tile = rows_dev // n_col
    per_level = n_row * n_col
    offset = 0
    update = None
    panel_list = []
    for level_k in range(levels):
        group = 2**level_k
        width = group * n_row * tile
        block = initials[:, 0, offset : offset + width]
        offset = offset + width
        local_level = lvl % group
        front_q = lvl // group
        row_tiles = per_level * lvl + n_col * row_idx + jnp.arange(n_col)
        col_tiles = front_q * per_level * group + n_col * jnp.arange(group * n_row) + col_idx
        label_rows = lax.dynamic_slice_in_dim(
            patches[level_k], per_level * lvl + n_col * row_idx, n_col
        )
        label_cols = pick_column(
            patches[level_k], front_q * per_level * group, group * n_row, n_col, col_idx
        )
        coupled = (jnp.abs(label_rows[:, None] - label_cols[None, :]) <= 1) | (
            row_tiles[:, None] == col_tiles[None, :]
        )
        cells = jnp.repeat(jnp.repeat(coupled.astype(jnp.float32), tile, axis=0), tile, axis=1)
        front = block * cells
        if level_k > 0:
            child = group // 2
            side = lvl // child % 2
            partner_lvl = lvl + child - 2 * child * side
            partner_update = from_partner(update, "level", level_k - 1)
            hvec = halves[level_k - 1]
            own_rows = lax.dynamic_slice_in_dim(hvec, per_level * lvl + n_col * row_idx, n_col)
            other_rows = lax.dynamic_slice_in_dim(
                hvec, per_level * partner_lvl + n_col * row_idx, n_col
            )
            own_cols = pick_column(
                hvec, lvl // child * per_level * child, child * n_row, n_col, col_idx
            )
            other_cols = pick_column(
                hvec, partner_lvl // child * per_level * child, child * n_row, n_col, col_idx
            )
            front = front + place_update(update, own_rows, own_cols, side, tile)
            front = front + place_update(partner_update, other_rows, other_cols, side, tile)
        pivot_cols = front[:, :tile]
        rows_piv = lax.all_gather(pivot_cols, "col", axis=1, tiled=True)
        piece = lax.dynamic_slice_in_dim(rows_piv, col_idx * tile, tile, 0)
        if level_k == 0:
            column_rows = lax.all_gather(piece, "row", axis=0, tiled=True)
        else:
            gathered = lax.all_gather(piece, ("level", "row"), axis=0, tiled=True)
            column_rows = lax.dynamic_slice_in_dim(
                gathered, (lvl - local_level) * n_row * tile, group * n_row * tile, 0
            )
        pivot_block = lax.all_gather(column_rows[:tile], "col", axis=0, tiled=True)
        factor = jnp.linalg.cholesky(pivot_block)
        panel_rows = jax.scipy.linalg.solve_triangular(factor, rows_piv.T, lower=True).T
        panel_cols = jax.scipy.linalg.solve_triangular(factor, column_rows.T, lower=True).T
        schur = front - jnp.dot(
            panel_rows,
            panel_cols.T,
            precision=lax.Precision.HIGHEST,
            preferred_element_type=jnp.float32,
        )
        row_flag = 1.0 - ((local_level == 0) & (row_idx == 0)).astype(jnp.float32)
        col_keep = (jnp.arange(width) >= tile).astype(jnp.float32)
        update = schur * row_flag * col_keep[None, :]
        panel_list.append(lax.dynamic_slice_in_dim(panel_rows, col_idx * tile, tile, 1))
    return (jnp.stack(panel_list, axis=0), update[:, None, :])


def solution(mesh):
    placed = (P(("level", "row"), "col", None), P(), P())
    return jax.shard_map(
        local,
        mesh=mesh,
        in_specs=placed,
        out_specs=(P(None, ("level", "row"), "col"), P(("level", "row"), "col", None)),
        check_vma=False,
    )
```

profile of v0, /device:TPU:0, one launch (start us, length us, event | category | flops | bytes accessed | tf_op | source)
XLA Modules:
  0.0 537.8 jit_solution(3740675650264493974)
XLA Ops:
  11.8 30.7 %all-gather.7.cloned.1.call-done = f32[512,512]{0,1:T(8,128)} async-done(((f32[512,128]{0,1:T(8,128)}), f32[512,512]{0,1:T(8,128)}) %all-gather.7.cloned.1.call-update) | async-done | bytes 1048592 | tf_op jit(solution)/shard_map/all_gather | solution.py:80
  42.5 1.7 constant_dynamic-slice_fusion.8
  44.3 16.8 %all-gather.9.cloned.1.call-done = f32[512,512]{0,1:T(8,128)} async-done(((f32[128,512]{0,1:T(8,128)}), f32[512,512]{0,1:T(8,128)}) %all-gather.9.cloned.1.call-update) | async-done | bytes 1048592 | tf_op jit(solution)/shard_map/all_gather | solution.py:83
  61.0 1.7 slice.174
  63.1 30.3 %all-gather.11.cloned.1.call-done = f32[512,512]{0,1:T(8,128)} async-done(((f32[128,512]{0,1:T(8,128)}), f32[512,512]{0,1:T(8,128)}) %all-gather.11.cloned.1.call-update) | async-done | bytes 1048592 | tf_op jit(solution)/shard_map/all_gather | solution.py:89
  96.3 11.7 %cholesky.286 = f32[128,128]{1,0:T(8,128)S(1)} custom-call(f32[128,128]{1,0:T(8,128)S(1)} %cholesky.426), custom_call_target="Cholesky" | custom-call | tf_op jit(solution)/shard_map/jit(cholesky)/cholesky | solution.py:90
  108.7 9.8 %custom-call.33 = f32[1,128,128]{1,2,0:T(8,128)S(1)} custom-call(f32[1,128,128]{2,1,0:T(8,128)S(1)} %get-tuple-element.87), custom_call_target="InvertDiagBlocksLowerTriangular" | custom-call | tf_op jit(solution)/shard_map/jit(cholesky)/cholesky | solution.py:90
  121.1 11.7 %cholesky.305 = f32[128,128]{1,0:T(8,128)S(1)} custom-call(f32[128,128]{1,0:T(8,128)S(1)} %cholesky.430), custom_call_target="Cholesky" | custom-call | tf_op jit(solution)/shard_map/jit(cholesky)/cholesky | solution.py:90
  133.5 10.1 %custom-call.34 = f32[1,128,128]{1,2,0:T(8,128)S(1)} custom-call(f32[1,128,128]{2,1,0:T(8,128)S(1)} %get-tuple-element.84), custom_call_target="InvertDiagBlocksLowerTriangular" | custom-call | tf_op jit(solution)/shard_map/jit(cholesky)/cholesky | solution.py:90
  145.2 11.7 %cholesky.326 = f32[128,128]{1,0:T(8,128)S(1)} custom-call(f32[128,128]{1,0:T(8,128)S(1)} %cholesky.435), custom_call_target="Cholesky" | custom-call | tf_op jit(solution)/shard_map/jit(cholesky)/cholesky | solution.py:90
  157.6 9.8 %custom-call.35 = f32[1,128,128]{1,2,0:T(8,128)S(1)} custom-call(f32[1,128,128]{2,1,0:T(8,128)S(1)} %get-tuple-element.81), custom_call_target="InvertDiagBlocksLowerTriangular" | custom-call | tf_op jit(solution)/shard_map/jit(cholesky)/cholesky | solution.py:90
  168.9 11.7 %cholesky.343 = f32[128,128]{1,0:T(8,128)S(1)} custom-call(f32[128,128]{1,0:T(8,128)S(1)} %convolution_subtract_fusion.17), custom_call_target="Cholesky" | custom-call | tf_op jit(solution)/shard_map/jit(cholesky)/cholesky | solution.py:90
  184.1 8.0 %while.7 = (s32[]{:T(128)}, f32[512,512]{1,0:T(8,128)S(1)}, s32[4,2]{0,1:T(2,128)S(1)}, f32[4,128,128]{2,1,0:T(8,128)S(1)}, s32[]{:T(128)}) while((s32[]{:T(128)}, f32[512,512]{1,0:T(8,128)S(1)}, s32[4,2]{0,1:T(2,128)S(1)}, f32[4,128,128]{2,1,0:T(8,128)S(1)}, s32[]{:T(128)}) %tuple.75), condition=%wide.while_cond, body=%wide.while_body.sunk | while | flops 2 | bytes 131189 | solution.py:91
  192.1 39.3 %custom-call.36 = f32[4,128,128]{1,2,0:T(8,128)S(1)} custom-call(f32[4,128,128]{2,1,0:T(8,128)S(1)} %get-tuple-element.32), custom_call_target="InvertDiagBlocksLowerTriangular" | custom-call | tf_op jit(solution)/shard_map/jit(_solve_triangular)/triangular_solve | solution.py:91
  244.4 3.8 broadcast_multiply_fusion.3
  250.2 4.4 copy.21
  255.0 17.3 %collective-permute-done = f32[512,512]{0,1:T(8,128)} collective-permute-done((f32[512,512]{0,1:T(8,128)}, f32[512,512]{0,1:T(8,128)}, u32[]{:S(2)}, u32[]{:S(2)}) %collective-permute-start) | collective-permute-done | bytes 1048608 | tf_op jit(solution)/shard_map/ppermute | solution.py:10
  273.8 2.0 fusion.1
  277.9 27.2 %all-gather.13.cloned.1.call-done = f32[512,512]{0,1:T(8,128)} async-done(((f32[512,128]{0,1:T(8,128)}), f32[512,512]{0,1:T(8,128)}) %all-gather.13.cloned.1.call-update) | async-done | bytes 1048592 | tf_op jit(solution)/shard_map/all_gather | solution.py:80
  307.1 28.1 %all-gather.15.cloned.1.call-done = f32[1024,512]{0,1:T(8,128)} async-done(((f32[128,512]{0,1:T(8,128)}), f32[1024,512]{0,1:T(8,128)}) %all-gather.15.cloned.1.call-update) | async-done | bytes 2097168 | tf_op jit(solution)/shard_map/all_gather | solution.py:85
  337.7 29.7 %all-gather.17.cloned.1.call-done = f32[512,512]{0,1:T(8,128)} async-done(((f32[128,512]{0,1:T(8,128)}), f32[512,512]{0,1:T(8,128)}) %all-gather.17.cloned.1.call-update) | async-done | bytes 1048592 | tf_op jit(solution)/shard_map/all_gather | solution.py:89
  369.3 11.7 %cholesky.358 = f32[128,128]{1,0:T(8,128)S(1)} custom-call(f32[128,128]{1,0:T(8,128)S(1)} %cholesky.439), custom_call_target="Cholesky" | custom-call | tf_op jit(solution)/shard_map/jit(cholesky)/cholesky | solution.py:90
  381.7 9.8 %custom-call.38 = f32[1,128,128]{1,2,0:T(8,128)S(1)} custom-call(f32[1,128,128]{2,1,0:T(8,128)S(1)} %get-tuple-element.77), custom_call_target="InvertDiagBlocksLowerTriangular" | custom-call | tf_op jit(solution)/shard_map/jit(cholesky)/cholesky | solution.py:90
  392.3 11.7 %cholesky.377 = f32[128,128]{1,0:T(8,128)S(1)} custom-call(f32[128,128]{1,0:T(8,128)S(1)} %cholesky.443), custom_call_target="Cholesky" | custom-call | tf_op jit(solution)/shard_map/jit(cholesky)/cholesky | solution.py:90
  404.7 10.2 %custom-call.39 = f32[1,128,128]{1,2,0:T(8,128)S(1)} custom-call(f32[1,128,128]{2,1,0:T(8,128)S(1)} %get-tuple-element.74), custom_call_target="InvertDiagBlocksLowerTriangular" | custom-call | tf_op jit(solution)/shard_map/jit(cholesky)/cholesky | solution.py:90
  415.5 11.7 %cholesky.398 = f32[128,128]{1,0:T(8,128)S(1)} custom-call(f32[128,128]{1,0:T(8,128)S(1)} %cholesky.448), custom_call_target="Cholesky" | custom-call | tf_op jit(solution)/shard_map/jit(cholesky)/cholesky | solution.py:90
  427.9 9.8 %custom-call.40 = f32[1,128,128]{1,2,0:T(8,128)S(1)} custom-call(f32[1,128,128]{2,1,0:T(8,128)S(1)} %get-tuple-element.71), custom_call_target="InvertDiagBlocksLowerTriangular" | custom-call | tf_op jit(solution)/shard_map/jit(cholesky)/cholesky | solution.py:90
  438.4 11.9 %cholesky.415 = f32[128,128]{1,0:T(8,128)S(1)} custom-call(f32[128,128]{1,0:T(8,128)S(1)} %convolution_subtract_fusion.16), custom_call_target="Cholesky" | custom-call | tf_op jit(solution)/shard_map/jit(cholesky)/cholesky | solution.py:90
  453.7 7.6 %while.8 = (s32[]{:T(128)}, f32[512,512]{1,0:T(8,128)S(1)}, s32[4,2]{0,1:T(2,128)S(1)}, f32[4,128,128]{2,1,0:T(8,128)S(1)}, s32[]{:T(128)}) while((s32[]{:T(128)}, f32[512,512]{1,0:T(8,128)S(1)}, s32[4,2]{0,1:T(2,128)S(1)}, f32[4,128,128]{2,1,0:T(8,128)S(1)}, s32[]{:T(128)}) %tuple.93), condition=%wide.while_cond.clone.1, body=%wide.while_body.clone.1.sunk | while | flops 2 | bytes 131189 | solution.py:91
  461.3 39.3 %custom-call.41 = f32[4,128,128]{1,2,0:T(8,128)S(1)} custom-call(f32[4,128,128]{2,1,0:T(8,128)S(1)} %get-tuple-element.34), custom_call_target="InvertDiagBlocksLowerTriangular" | custom-call | tf_op jit(solution)/shard_map/jit(_solve_triangular)/triangular_solve | solution.py:91
  515.1 9.6 %multiply_bitcast_fusion = f32[512,1,1024]{0,2,1:T(8,128)} fusion(f32[512,1024]{0,1:T(8,128)} %copy-done.7, f32[128,1024]{1,0:T(8,128)} %fusion.107, f32[128,1024]{1,0:T(8,128)S(1)} %fusion.105, f32[128,1024]{1,0:T(8,128)S(1)} %fusion.103, f32[128,1024]{1,0:T(8,128)S(1)} %fusion.50, f32[1024]{0:T(1024)S(1)} %fusion.113, f32[]{:T(128)S(6)} %sub.83, ...), kind=kOutput, calls=%fused_computation.17 | convolution fusion | flops 3225157632 | bytes 7344132 | tf_op jit(solution)/shard_map/dot_general | solution.py:93
  524.7 6.0 %copy.18 = f32[512,1,1024]{2,1,0:T(1,128)} copy(f32[512,1,1024]{0,2,1:T(8,128)} %multiply_bitcast_fusion) | data formatting | bytes 4194304
  (185 shorter events, 76.1 us)
Async XLA Ops:
  7.2 2.3 slice-start
  7.2 35.3 %all-gather.7.cloned.1.call-start = ((), (), s32[]{:S(2)}) async-start(), calls=%async_computation | async-start | bytes 1310720 | tf_op jit(solution)/shard_map/all_gather | solution.py:80
  10.8 52.0 %copy-start.14 = (s32[1,32]{1,0:T(1,128)S(1)}, s32[1,32]{1,0:T(1,128)}, u32[]{:S(2)}) copy-start(s32[1,32]{1,0:T(1,128)} %param.8) | copy-start | bytes 388
  11.7 49.3 %all-gather.9.cloned.1.call-start = ((), (), s32[]{:S(2)}) async-start(), calls=%async_computation.1 | async-start | bytes 1310720 | tf_op jit(solution)/shard_map/all_gather | solution.py:83
  44.2 49.2 %all-gather.11.cloned.1.call-start = ((), (), s32[]{:S(2)}) async-start(), calls=%async_computation.2 | async-start | bytes 1310720 | tf_op jit(solution)/shard_map/all_gather | solution.py:89
  62.7 242.5 %all-gather.13.cloned.1.call-start = ((), (), s32[]{:S(2)}) async-start(), calls=%async_computation.3 | async-start | bytes 1310720 | tf_op jit(solution)/shard_map/all_gather | solution.py:80
  93.4 1.7 copy-start.2
  95.3 1.0 copy-start.5
  192.1 47.7 %copy-start.1 = (f32[512,512]{1,0:T(8,128)}, f32[512,512]{1,0:T(8,128)S(1)}, u32[]{:S(2)}) copy-start(f32[512,512]{1,0:T(8,128)S(1)} %get-tuple-element.200) | copy-start | bytes 3145732
  235.6 4.3 copy-start.8
  248.2 24.1 %collective-permute-start = (f32[512,512]{0,1:T(8,128)}, f32[512,512]{0,1:T(8,128)}, u32[]{:S(2)}, u32[]{:S(2)}) collective-permute-start(f32[512,512]{0,1:T(8,128)} %get-tuple-element.95), channel_id=1, source_target_pairs={{0,16},{16,0},{1,17},{17,1},{2,18},{18,2},{3,19},{19,3},{4,20},{20... | collective-permute-start | bytes 3145736 | tf_op jit(solution)/shard_map/ppermute | solution.py:10
  248.6 1.6 slice-start.1
  254.6 19.1 %copy-start = (f32[512,1,1024]{0,2,1:T(8,128)S(1)}, f32[512,1,1024]{0,2,1:T(8,128)}, u32[]{:S(2)}) copy-start(f32[512,1,1024]{0,2,1:T(8,128)} %copy.21) | copy-start | bytes 6291460
  254.6 19.1 %copy-start.4 = (f32[512,512]{0,1:T(8,128)S(1)}, f32[512,512]{0,1:T(8,128)}, u32[]{:S(2)}) copy-start(f32[512,512]{0,1:T(8,128)} %get-tuple-element.66) | copy-start | bytes 3145732
  275.8 1.3 copy-start.7
  277.9 57.3 %all-gather.15.cloned.1.call-start = ((), (), s32[]{:S(2)}) async-start(), calls=%async_computation.4 | async-start | bytes 2359296 | tf_op jit(solution)/shard_map/all_gather | solution.py:85
  306.9 60.5 %all-gather.17.cloned.1.call-start = ((), (), s32[]{:S(2)}) async-start(), calls=%async_computation.5 | async-start | bytes 1310720 | tf_op jit(solution)/shard_map/all_gather | solution.py:89
  367.4 1.7 copy-start.3
  500.6 8.5 %copy-start.9 = (f32[4,128,128]{1,2,0:T(8,128)}, f32[4,128,128]{1,2,0:T(8,128)S(1)}, u32[]{:S(2)}) copy-start(f32[4,128,128]{1,2,0:T(8,128)S(1)} %custom-call.41) | copy-start | bytes 786436
  503.4 4.5 copy-start.6
  507.9 6.0 %copy-start.12 = (f32[128,512]{1,0:T(8,128)}, f32[128,512]{1,0:T(8,128)S(1)}, u32[]{:S(2)}) copy-start(f32[128,512]{1,0:T(8,128)S(1)} %fusion.108) | copy-start | bytes 786436
  509.8 1.0 copy-start.10
  512.5 1.6 copy-start.11
  514.0 1.1 copy-start.13
Sparse Core Ops, SparseCore 0:
  11.9 30.6 all-gather.6
  44.6 16.3 all-gather.8
  63.2 30.1 all-gather.10
  278.0 27.1 all-gather.12
  307.5 27.6 all-gather.14
  337.2 30.1 all-gather.16
where the time goes:
time: 548 us; the launch traced here: 538 us
  other arithmetic  243 us (44%)
  waiting for transfers between devices  180 us (33%)
  local copies, waits for them, and re-layouts  47.1 us (9%)
  matrix products  46.5 us (8%)
  between operations  20.2 us (4%)
    another operation x30, other arithmetic, local(): factor = jnp.linalg.cholesky(pivot_block)  159 us
    another operation x7, other arithmetic, local(): jax.scipy.linalg.solve_triangular(factor, rows_piv.T, lower=True)  79 us
    all_gather x2, waiting for transfers between devices, local(): pivot_block = lax.all_gather(column_rows[:tile], 'col', axis=0, tiled=True)  60 us
    all_gather x2, waiting for transfers between devices, local(): rows_piv = lax.all_gather(pivot_cols, 'col', axis=1, tiled=True)  58 us
    all_gather x1, waiting for transfers between devices, local(): gathered = lax.all_gather(piece, ('level', 'row'), axis=0, tiled=True)  28.1 us
    ppermute x1, waiting for transfers between devices, from_partner(): return lax.ppermute(value, axis, pairs)  17.3 us
    all_gather x1, waiting for transfers between devices, local(): column_rows = lax.all_gather(piece, 'row', axis=0, tiled=True)  16.8 us
    another operation x27, local copies, waits for them, and re-layouts, local(): jax.scipy.linalg.solve_triangular(factor, rows_piv.T, lower=True)  15.5 us
  transfers between devices with their start and end apart: 7, of which 7 were waited for; matrix products, arithmetic and copies ran while one was open for 1% of the time, Pallas kernels for 0%

commit v1 on v0

v1 whole, which is shorter than its diff:
```python
import functools

import jax
import jax.numpy as jnp
from jax import lax
from jax.experimental import pallas as pl
from jax.experimental.pallas import tpu as pltpu
from jax.sharding import PartitionSpec as P

HIGHEST = lax.Precision.HIGHEST


def from_partner(value, axis, bit):
    mask = 2**bit
    pairs = [(source, source ^ mask) for source in range(lax.axis_size(axis))]
    return lax.ppermute(value, axis, pairs)


def pick_column(vector, start, count_j, n_col, col_idx):
    segment = lax.dynamic_slice_in_dim(vector, start, count_j * n_col).reshape(count_j, n_col)
    onehot = jnp.arange(n_col) == col_idx
    return jnp.sum(jnp.where(onehot[None, :], segment, 0), axis=1)


def place_update(update, row_half, col_half, side, tile):
    row_keep = jnp.repeat(row_half == side, tile)
    col_high = jnp.repeat(col_half == 1, tile)
    lower_part = jnp.where(row_keep[:, None] & ~col_high[None, :], update, 0.0)
    upper_part = jnp.where(row_keep[:, None] & col_high[None, :], update, 0.0)
    return jnp.concatenate([lower_part, upper_part], axis=1)


def spread_lane(value, lane):
    return jnp.broadcast_to(value[:, lane : lane + 1], value.shape)


def inverse_factor(blocks):
    n = blocks[0].shape[0]
    lane = lax.broadcasted_iota(jnp.int32, (8, n), 1)
    sub = lax.broadcasted_iota(jnp.int32, (8, n), 0)
    states = [[block[8 * v : 8 * v + 8] for v in range(n // 8)] for block in blocks]
    results = [[] for _ in blocks]
    for step in range(n // 8):
        first = 8 * step
        inside = (lane >= first) & (lane < first + 8)
        for rows, done in zip(states, results):
            head = rows[step]
            row = [jnp.broadcast_to(head[j : j + 1], (8, n)) for j in range(8)]
            small = {(i, j): spread_lane(row[j], first + i) for j in range(8) for i in range(j, 8)}
            hat = [
                jnp.where(inside, jnp.where(lane == first + j, 1.0, 0.0), row[j]) for j in range(8)
            ]
            inv = []
            mult = {}
            for j in range(8):
                inv.append(1.0 / small[j, j])
                for i in range(j + 1, 8):
                    mult[i, j] = small[i, j] * inv[j]
                for i in range(j + 1, 8):
                    for m in range(j + 1, i + 1):
                        small[i, m] = small[i, m] - mult[i, j] * small[m, j]
                    hat[i] = hat[i] - mult[i, j] * hat[j]
            own = jnp.zeros((8, n), jnp.float32)
            for j in range(8):
                pivot = small[j, j]
                root = lax.rsqrt(pivot)
                root = root * (1.5 - 0.5 * pivot * root * root)
                own = jnp.where(sub == j, hat[j] * root, own)
            done.append(jnp.where(lane <= sub + first, own, 0.0))
            back = [None] * 8
            for i in range(7, -1, -1):
                value = hat[i] * inv[i]
                for j in range(i + 1, 8):
                    value = value - mult[j, i] * back[j]
                back[i] = value
            for v in range(step + 1, n // 8):
                parts = [spread_lane(rows[v], first + i) * back[i] for i in range(8)]
                while len(parts) > 1:
                    parts = [a + b for a, b in zip(parts[::2], parts[1::2])]
                rows[v] = jnp.where(inside, 0.0, rows[v]) - parts[0]
    return [jnp.concatenate(done, axis=0) for done in results]


def invert_kernel(a_ref, out_ref):
    fronts, pivots, _ = a_ref.shape
    tile = 128
    out_ref[...] = a_ref[...]
    col = lax.broadcasted_iota(jnp.int32, (tile, pivots), 1)
    big_col = lax.broadcasted_iota(jnp.int32, (pivots, pivots), 1)
    big_row = lax.broadcasted_iota(jnp.int32, (pivots, pivots), 0)

    def body(b, carry):
        start = pl.multiple_of(b * tile, tile)
        here = pl.ds(start, tile)
        diag = inverse_factor([out_ref[f, here, here] for f in range(fronts)])
        for f in range(fronts):
            row = jnp.dot(
                diag[f], out_ref[f, here, :], precision=HIGHEST, preferred_element_type=jnp.float32
            )
            inside = (col >= start) & (col < start + tile)
            wide = jnp.concatenate([diag[f]] * (pivots // tile), axis=1)
            row = jnp.where(inside, wide, row)
            below = jnp.where(col >= start + tile, row, 0.0)
            change = lax.dot_general(
                below,
                row,
                (((0,), (0,)), ((), ())),
                precision=HIGHEST,
                preferred_element_type=jnp.float32,
            )
            clear = (big_col >= start) & (big_col < start + tile) & (big_row >= start + tile)
            out_ref[f] = jnp.where(clear, 0.0, out_ref[f]) - change
            out_ref[f, here, :] = jnp.where(col < start + tile, row, 0.0)
        return carry

    lax.fori_loop(0, pivots // tile, body, 0)


def invert(pivot_blocks):
    return pl.pallas_call(
        invert_kernel,
        out_shape=jax.ShapeDtypeStruct(pivot_blocks.shape, jnp.float32),
        in_specs=[pl.BlockSpec(memory_space=pltpu.VMEM)],
        out_specs=pl.BlockSpec(memory_space=pltpu.VMEM),
        compiler_params=pltpu.CompilerParams(vmem_limit_bytes=40 * 2**20),
        cost_estimate=pl.CostEstimate(flops=60 * 10**9, bytes_accessed=4 * 2**20, transcendentals=0),
    )(pivot_blocks)


def dot(a, b, contract):
    return lax.dot_general(
        a, b, ((contract), ((), ())), precision=HIGHEST, preferred_element_type=jnp.float32
    )


def local(initials, patches, halves):
    n_level = lax.axis_size("level")
    n_row = lax.axis_size("row")
    n_col = lax.axis_size("col")
    levels = n_level.bit_length()
    lvl = lax.axis_index("level")
    row_idx = lax.axis_index("row")
    col_idx = lax.axis_index("col")
    rows_dev = initials.shape[0]
    tile = rows_dev // n_col
    per_level = n_row * n_col
    offset = 0
    fronts = []
    for level_k in range(levels):
        group = 2**level_k
        width = group * n_row * tile
        block = initials[:, 0, offset : offset + width]
        offset = offset + width
        front_q = lvl // group
        row_tiles = per_level * lvl + n_col * row_idx + jnp.arange(n_col)
        col_tiles = front_q * per_level * group + n_col * jnp.arange(group * n_row) + col_idx
        label_rows = lax.dynamic_slice_in_dim(
            patches[level_k], per_level * lvl + n_col * row_idx, n_col
        )
        label_cols = pick_column(
            patches[level_k], front_q * per_level * group, group * n_row, n_col, col_idx
        )
        coupled = (jnp.abs(label_rows[:, None] - label_cols[None, :]) <= 1) | (
            row_tiles[:, None] == col_tiles[None, :]
        )
        cells = jnp.repeat(jnp.repeat(coupled, tile, axis=0), tile, axis=1)
        fronts.append(jnp.where(cells, block, 0.0))

    pivot_cols = jnp.stack([front[:, :tile] for front in fronts], axis=0)
    rows_piv = lax.all_gather(pivot_cols, "col", axis=2, tiled=True)
    piece = lax.dynamic_slice_in_dim(rows_piv, col_idx * tile, tile, 1)
    gathered = lax.all_gather(piece, ("level", "row"), axis=1, tiled=True)
    column_rows = []
    for level_k in range(levels):
        group = 2**level_k
        column_rows.append(
            lax.dynamic_slice_in_dim(
                gathered[level_k], lvl // group * group * n_row * tile, group * n_row * tile, 0
            )
        )
    heads = jnp.stack([rows[:tile] for rows in column_rows], axis=0)
    pivot_blocks = lax.all_gather(heads, "col", axis=1, tiled=True)
    inverses = invert(pivot_blocks)

    update = None
    panel_list = []
    for level_k in range(levels):
        group = 2**level_k
        width = group * n_row * tile
        local_level = lvl % group
        front = fronts[level_k]
        panel_rows = dot(rows_piv[level_k], inverses[level_k], ((1,), (1,)))
        panel_cols = dot(inverses[level_k], column_rows[level_k], ((1,), (1,)))
        schur = front - dot(panel_rows, panel_cols, ((1,), (0,)))
        if level_k > 0:
            child = group // 2
            side = lvl // child % 2
            partner_lvl = lvl + child - 2 * child * side
            partner_update = from_partner(update, "level", level_k - 1)
            hvec = halves[level_k - 1]
            own_rows = lax.dynamic_slice_in_dim(hvec, per_level * lvl + n_col * row_idx, n_col)
            other_rows = lax.dynamic_slice_in_dim(
                hvec, per_level * partner_lvl + n_col * row_idx, n_col
            )
            own_cols = pick_column(
                hvec, lvl // child * per_level * child, child * n_row, n_col, col_idx
            )
            other_cols = pick_column(
                hvec, partner_lvl // child * per_level * child, child * n_row, n_col, col_idx
            )
            schur = schur + place_update(update, own_rows, own_cols, side, tile)
            schur = schur + place_update(partner_update, other_rows, other_cols, side, tile)
        keep_row = ~((local_level == 0) & (row_idx == 0))
        keep_col = jnp.arange(width) >= tile
        update = jnp.where(keep_row & keep_col[None, :], schur, 0.0)
        panel_list.append(lax.dynamic_slice_in_dim(panel_rows, col_idx * tile, tile, 1))
    return (jnp.stack(panel_list, axis=0), update[:, None, :])


def solution(mesh):
    placed = (P(("level", "row"), "col", None), P(), P())
    return jax.shard_map(
        local,
        mesh=mesh,
        in_specs=placed,
        out_specs=(P(None, ("level", "row"), "col"), P(("level", "row"), "col", None)),
        check_vma=False,
    )
```

time: 548 us -> 250 us (0.46); the launches traced: 538 us -> 249 us
  other arithmetic: 243 us -> 7.36 us
  Pallas kernels: 0 us -> 41.6 us
  waiting for transfers between devices: 180 us -> 147 us
  matrix products: 46.5 us -> 15 us
  local copies, waits for them, and re-layouts: 47.1 us -> 22.5 us
  between operations: 20.2 us -> 14 us
    another operation x37 -> x2, other arithmetic: 238 us -> 1.66 us  [the longest x1 0.83 us: local(): heads = jnp.stack([rows[:tile] for rows in column_rows], axis=0)]
    pallas_call x0 -> x1, Pallas kernels: none -> 41.6 us  [invert(): pl.pallas_call(invert_kernel, out_shape=jax.ShapeDtypeStruct(pivot_blocks...]
    another operation x40 -> x0, matrix products: 33.1 us -> none  [the longest x14 13.1 us: local(): jax.scipy.linalg.solve_triangular(factor, rows_piv.T, lower=True)]
    all_gather x6 -> x3, waiting for transfers between devices: 163 us -> 130 us  [the longest x1 49 us: local(): rows_piv = lax.all_gather(pivot_cols, 'col', axis=2, tiled=True)]
    another operation x35 -> x4, local copies, waits for them, and re-layouts: 15.7 us -> 0.22 us  [the longest x2 0.15 us: place_update(): lower_part = jnp.where(row_keep[:, None] & ~col_high[None, :], update, 0.0)]
    unnamed x36 -> x15, local copies, waits for them, and re-layouts: 15.4 us -> 6.4 us
    slice x4 -> x2, local copies, waits for them, and re-layouts: 1.52 us -> 7.28 us  [local(): block = initials[:, 0, offset:offset + width]]
    dot_general x2 -> x6, matrix products: 13.4 us -> 15 us  [dot(): lax.dot_general(a, b, (contract, ((), ())), precision=HIGHEST, preferred_...]
  transfers between devices with their start and end apart: 7 -> 4, of which waited for: 7 -> 4; matrix products, arithmetic and copies ran while one was open for 1% -> 3% of each run, Pallas kernels for 0% -> 0%
where the time goes in v1:
time: 250 us; the launch traced here: 249 us
  waiting for transfers between devices  147 us (59%)
  Pallas kernels  41.6 us (17%)
  local copies, waits for them, and re-layouts  22.5 us (9%)
  matrix products  15 us (6%)
  between operations  14 us (6%)
  other arithmetic  7.36 us (3%)
    all_gather x1, waiting for transfers between devices, local(): rows_piv = lax.all_gather(pivot_cols, 'col', axis=2, tiled=True)  49 us
    all_gather x1, waiting for transfers between devices, local(): pivot_blocks = lax.all_gather(heads, 'col', axis=1, tiled=True)  45.5 us
    pallas_call x1, Pallas kernels, invert(): pl.pallas_call(invert_kernel, out_shape=jax.ShapeDtypeStruct(pivot_blocks...  41.6 us
    all_gather x1, waiting for transfers between devices, local(): gathered = lax.all_gather(piece, ('level', 'row'), axis=1, tiled=True)  35.3 us
    ppermute x1, waiting for transfers between devices, from_partner(): return lax.ppermute(value, axis, pairs)  17 us
    dot_general x6, matrix products, dot(): lax.dot_general(a, b, (contract, ((), ())), precision=HIGHEST, preferred_...  15 us
    slice x2, local copies, waits for them, and re-layouts, local(): block = initials[:, 0, offset:offset + width]  7.28 us
    unnamed x15, local copies, waits for them, and re-layouts  6.4 us
  transfers between devices with their start and end apart: 4, of which 4 were waited for; matrix products, arithmetic and copies ran while one was open for 3% of the time, Pallas kernels for 0%

profile of v1, /device:TPU:0, one launch (start us, length us, event | category | flops | bytes accessed | tf_op | source)
XLA Modules:
  0.0 249.2 jit_solution(3413201012548421049)
XLA Ops:
  7.3 4.4 %slice.53 = f32[512,1,1024]{2,1,0:T(1,128)} slice(f32[512,1,1536]{2,1,0:T(1,128)} %param.3), slice={[0:512], [0:1], [512:1536]} | slice | bytes 4194304 | tf_op jit(solution)/shard_map/slice | solution.py:152
  11.6 2.9 %slice.50 = f32[512,1,512]{2,1,0:T(1,128)} slice(f32[512,1,1536]{2,1,0:T(1,128)} %param.3), slice={[0:512], [0:1], [0:512]} | slice | bytes 2097152 | tf_op jit(solution)/shard_map/slice | solution.py:152
  14.7 0.1 select_reduce_fusion
  15.0 1.6 broadcast_in_dim.113
  16.6 2.2 fusion.4
  18.9 0.1 fusion.21
  19.2 0.2 select_reduce_fusion.1
  19.5 1.6 broadcast_in_dim.108
  21.1 1.4 fusion.8
  22.6 0.8 pad_maximum_fusion
  23.5 49.0 %all-gather.4.cloned.1.call-done = f32[2,512,512]{2,1,0:T(8,128)} async-done(((f32[2,512,128]{2,1,0:T(8,128)}), f32[2,512,512]{2,1,0:T(8,128)}) %all-gather.4.cloned.1.call-update) | async-done | bytes 2097168 | tf_op jit(solution)/shard_map/all_gather | solution.py:170
  72.5 1.9 constant_dynamic-slice_fusion.5
  74.4 0.2 all-gather.8.cloned.1.call-start
  74.6 35.3 %all-gather.6.cloned.1.call-done = f32[2,1024,512]{2,1,0:T(8,128)} async-done(((f32[2,128,512]{2,1,0:T(8,128)}), f32[2,1024,512]{2,1,0:T(8,128)}) %all-gather.6.cloned.1.call-update) | async-done | bytes 4194320 | tf_op jit(solution)/shard_map/all_gather | solution.py:172
  110.0 1.8 slice.66
  111.7 1.3 copy-done.1
  113.1 1.0 slice.67
  114.0 0.8 pad_maximum_fusion.1
  115.5 45.5 %all-gather.8.cloned.1.call-done.a_ref = f32[2,512,512]{2,1,0:T(8,128)} async-done(((f32[2,128,512]{2,1,0:T(8,128)}), f32[2,512,512]{2,1,0:T(8,128)}) %all-gather.8.cloned.1.call-update) | async-done | bytes 2097168 | tf_op jit(solution)/shard_map/all_gather | solution.py:182
  161.0 1.6 copy-done
  162.6 41.6 %shard_map.50 = f32[2,512,512]{2,1,0:T(8,128)S(1)} custom-call(f32[2,512,512]{2,1,0:T(8,128)S(1)} %copy-done), custom_call_target="tpu_custom_call" | custom-call | flops 60000002048 | bytes 4194304 | tf_op jit(solution)/shard_map/pallas_call | solution.py:120
  204.2 1.9 fusion.9
  206.1 1.9 fusion.7
  208.0 2.1 and_select_fusion.3
  210.0 1.5 collective-permute-start
  211.6 1.9 fusion.6
  213.5 0.8 pad_maximum_fusion.2
  214.4 3.6 %fusion = f32[512,1024]{1,0:T(8,128)S(1)} fusion(f32[2,1024,512]{2,1,0:T(8,128)S(1)} %copy-done.3, f32[2,512,512]{2,1,0:T(8,128)S(1)} %shard_map.50), kind=kOutput, calls=%fused_computation.1 | convolution fusion | flops 3221225472 | bytes 5242880 | tf_op jit(solution)/shard_map/dot_general | solution.py:131
  218.0 17.0 %collective-permute-done = f32[512,512]{1,0:T(8,128)S(1)} collective-permute-done((f32[512,512]{1,0:T(8,128)S(1)}, f32[512,512]{1,0:T(8,128)S(1)}, u32[]{:S(2)}, u32[]{:S(2)}) %collective-permute-start) | collective-permute-done | bytes 1048608 | tf_op jit(solution)/shard_map/ppermute | solution.py:16
  235.0 0.5 and_select_fusion.1
  235.5 3.7 %fusion.3 = f32[512,1,1024]{2,0,1:T(8,128)S(1)} fusion(f32[512,512]{1,0:T(8,128)S(1)} %get-tuple-element.14, f32[512,512]{1,0:T(8,128)S(1)} %get-tuple-element.13, f32[512,512]{1,0:T(8,128)S(1)} %get-tuple-element.12, f32[512,512]{1,0:T(8,128)S(1)} %get-tuple-element.11, f32[512,1024]{1,0:T(8,128)S(1)} %fusion.4, f32[512,512]{1,0:T(8,128)S(1)} %fusion.6, ...), kind=kOutput, calls=%fused_computation.5 | convolution fusion | flops 3224371200 | bytes 11535360 | tf_op jit(solution)/shard_map/dot_general | solution.py:131
  239.2 3.5 %copy.12 = f32[512,1,1024]{2,1,0:T(1,128)} copy(f32[512,1,1024]{2,0,1:T(8,128)S(1)} %fusion.3) | data formatting | bytes 4194304
  (46 shorter events, 1.5 us)
Async XLA Ops:
  7.2 65.3 %all-gather.4.cloned.1.call-start = ((), (), s32[]{:S(2)}) async-start(), calls=%async_computation | async-start | bytes 2621440 | tf_op jit(solution)/shard_map/all_gather | solution.py:170
  11.6 2.9 %copy-start.6 = (s32[2,32]{1,0:T(2,128)S(1)}, s32[2,32]{1,0:T(2,128)}, u32[]{:S(2)}) copy-start(s32[2,32]{1,0:T(2,128)} %param.4) | copy-start | bytes 772
  16.6 2.3 copy-start.5
  23.4 86.6 %all-gather.6.cloned.1.call-start = ((), (), s32[]{:S(2)}) async-start(), calls=%async_computation.1 | async-start | bytes 4718592 | tf_op jit(solution)/shard_map/all_gather | solution.py:172
  74.4 86.6 %all-gather.8.cloned.1.call-start = ((), (), s32[]{:S(2)}) async-start(), calls=%async_computation.2 | async-start | bytes 2621440 | tf_op jit(solution)/shard_map/all_gather | solution.py:182
  111.7 1.3 copy-start.1
  161.0 1.6 copy-start
  162.6 41.6 %copy-start.2 = (f32[1,1024,512]{2,1,0:T(8,128)S(1)}, f32[1,1024,512]{2,1,0:T(8,128)}, u32[]{:S(2)}) copy-start(f32[1,1024,512]{2,1,0:T(8,128)} %copy-done.1) | copy-start | bytes 6291460
  204.2 1.9 copy-start.4
  210.0 24.9 %collective-permute-start = (f32[512,512]{1,0:T(8,128)S(1)}, f32[512,512]{1,0:T(8,128)S(1)}, u32[]{:S(2)}, u32[]{:S(2)}) collective-permute-start(f32[512,512]{1,0:T(8,128)S(1)} %get-tuple-element.20), channel_id=1, source_target_pairs={{0,16},{16,0},{1,17},{17,1},{2,18},{18,2},{3,19},{19,3},{4,20},{20... | collective-permute-start | bytes 3145736 | tf_op jit(solution)/shard_map/ppermute | solution.py:16
  211.6 2.8 %copy-start.3 = (f32[2,1024,512]{2,1,0:T(8,128)S(1)}, f32[2,1024,512]{2,1,0:T(8,128)}, u32[]{:S(2)}) copy-start(f32[2,1024,512]{2,1,0:T(8,128)} %all-gather.6.cloned.1.call-done) | copy-start | bytes 12582916
Sparse Core Ops, SparseCore 0:
  23.5 48.9 all-gather.3
  75.0 34.9 all-gather.5
  115.0 45.9 all-gather.7

commit v2 on v1

--- a/solution.py
+++ b/solution.py
@@ -81,10 +81,7 @@
     return [jnp.concatenate(done, axis=0) for done in results]
 
 
-def invert_kernel(a_ref, out_ref):
-    fronts, pivots, _ = a_ref.shape
-    tile = 128
-    out_ref[...] = a_ref[...]
+def eliminate(state, fronts, pivots, tile):
     col = lax.broadcasted_iota(jnp.int32, (tile, pivots), 1)
     big_col = lax.broadcasted_iota(jnp.int32, (pivots, pivots), 1)
     big_row = lax.broadcasted_iota(jnp.int32, (pivots, pivots), 0)
@@ -92,10 +89,10 @@
     def body(b, carry):
         start = pl.multiple_of(b * tile, tile)
         here = pl.ds(start, tile)
-        diag = inverse_factor([out_ref[f, here, here] for f in range(fronts)])
+        diag = inverse_factor([state[f, here, here] for f in range(fronts)])
         for f in range(fronts):
             row = jnp.dot(
-                diag[f], out_ref[f, here, :], precision=HIGHEST, preferred_element_type=jnp.float32
+                diag[f], state[f, here, :], precision=HIGHEST, preferred_element_type=jnp.float32
             )
             inside = (col >= start) & (col < start + tile)
             wide = jnp.concatenate([diag[f]] * (pivots // tile), axis=1)
@@ -109,22 +106,311 @@
                 preferred_element_type=jnp.float32,
             )
             clear = (big_col >= start) & (big_col < start + tile) & (big_row >= start + tile)
-            out_ref[f] = jnp.where(clear, 0.0, out_ref[f]) - change
-            out_ref[f, here, :] = jnp.where(col < start + tile, row, 0.0)
+            state[f] = jnp.where(clear, 0.0, state[f]) - change
+            state[f, here, :] = jnp.where(col < start + tile, row, 0.0)
         return carry
 
     lax.fori_loop(0, pivots // tile, body, 0)
 
 
-def invert(pivot_blocks):
-    return pl.pallas_call(
-        invert_kernel,
-        out_shape=jax.ShapeDtypeStruct(pivot_blocks.shape, jnp.float32),
-        in_specs=[pl.BlockSpec(memory_space=pltpu.VMEM)],
-        out_specs=pl.BlockSpec(memory_space=pltpu.VMEM),
-        compiler_params=pltpu.CompilerParams(vmem_limit_bytes=40 * 2**20),
+def gather_kernel(sizes, init_ref, lab_row_ref, lab_col_ref, inv_ref, rows_ref, *rest):
+    n_level, n_row, n_col, levels, tile = sizes
+    cols_refs = rest[:levels]
+    (
+        piv,
+        spread_send,
+        spread_recv,
+        line_send,
+        line_recv,
+        core_send,
+        core_recv,
+        row_send,
+        row_recv,
+        col_send,
+        col_recv,
+        own_piv,
+        own_rows,
+        own_cols,
+    ) = rest[levels:]
+    lvl = lax.axis_index("level")
+    row = lax.axis_index("row")
+    col = lax.axis_index("col")
+    pivots = n_col * tile
+    offsets = [(2**k - 1) * n_row * tile for k in range(levels)]
+
+    def remote(src, dst, send, recv, to):
+        return pltpu.make_async_remote_copy(
+            src_ref=src,
+            dst_ref=dst,
+            send_sem=send,
+            recv_sem=recv,
+            device_id=to,
+            device_id_type=pl.DeviceIdType.MESH,
+        )
+
+    def tiles(index):
+        return pl.ds(pl.multiple_of(index * tile, tile), tile)
+
+    def at_col(step):
+        return (lvl, row, lax.rem(col + step, n_col))
+
+    barrier = pltpu.get_barrier_semaphore()
+    greeted = 0
+    for step in range(1, n_col):
+        pl.semaphore_signal(
+            barrier, inc=1, device_id=at_col(step), device_id_type=pl.DeviceIdType.MESH
+        )
+        greeted += 1
+    for dl in range(n_level):
+        for dr in range(n_row):
+            if dl or dr:
+                peer = (lax.rem(lvl + dl, n_level), lax.rem(row + dr, n_row), col)
+                pl.semaphore_signal(
+                    barrier, inc=1, device_id=peer, device_id_type=pl.DeviceIdType.MESH
+                )
+                greeted += 1
+    pl.semaphore_wait(barrier, greeted)
+
+    def row_copy(k, step, slot):
+        target = lax.rem(col + step, n_col)
+        which = tiles(lax.rem(target + slot, n_col))
+        return remote(
+            init_ref.at[which, pl.ds(offsets[k], tile)],
+            rows_ref.at[k, which, tiles(col)],
+            row_send.at[k, step, slot],
+            row_recv.at[k, step, slot],
+            at_col(step),
+        )
+
+    def row_arrival(k, step, slot):
+        source = lax.rem(col + n_col - step, n_col)
+        which = tiles(lax.rem(col + slot, n_col))
+        return remote(
+            init_ref.at[which, pl.ds(offsets[k], tile)],
+            rows_ref.at[k, which, tiles(source)],
+            row_send.at[k, step, slot],
+            row_recv.at[k, step, slot],
+            at_col(step),
+        )
+
+    def piv_tile(k, step):
+        return piv.at[k, :, tiles(lax.rem(col + n_col - step, n_col))]
+
+    def line_copy(k, step):
+        return remote(
+            piv_tile(k, 0), piv_tile(k, 0), line_send.at[k, step], line_recv.at[k, step], at_col(step)
+        )
+
+    def line_arrival(k, step):
+        return remote(
+            piv_tile(k, step),
+            piv_tile(k, step),
+            line_send.at[k, step],
+            line_recv.at[k, step],
+            at_col(step),
+        )
+
+    def core_copy(k, step):
+        return remote(
+            piv_tile(k, step),
+            piv_tile(k, step),
+            core_send.at[k, step],
+            core_recv.at[k, step],
+            (lvl, row // 2 * 2 + 1 - lax.rem(row, 2), col),
+        )
+
+    def spread_copy(k, slot, dl, to_row):
+        return remote(
+            piv_tile(k, 0),
+            piv_tile(k, 0),
+            spread_send.at[k, slot],
+            spread_recv.at[k],
+            (lax.rem(lvl + dl, n_level), to_row, col),
+        )
+
+    def col_parts(k, dl, dr, sign):
+        group = 2**k
+        inner = lax.rem(lvl, group)
+        part_l = lax.rem(inner + (group + sign * dl), group)
+        part_r = lax.rem(row + (n_row + sign * dr), n_row)
+        return inner, part_l, part_r
+
+    def col_copy(k, dl, dr):
+        slot = dl * n_row + dr
+        inner, to_l, to_r = col_parts(k, dl, dr, 1)
+        return remote(
+            rows_ref.at[k, tiles(col), :],
+            cols_refs[k].at[tiles(inner * n_row + row), :],
+            col_send.at[k, slot],
+            col_recv.at[k, slot],
+            (lvl - inner + to_l, to_r, col),
+        )
+
+    def col_arrival(k, dl, dr):
+        slot = dl * n_row + dr
+        inner, to_l, to_r = col_parts(k, dl, dr, 1)
+        _, from_l, from_r = col_parts(k, dl, dr, -1)
+        return remote(
+            rows_ref.at[k, tiles(col), :],
+            cols_refs[k].at[tiles(from_l * n_row + from_r), :],
+            col_send.at[k, slot],
+            col_recv.at[k, slot],
+            (lvl - inner + to_l, to_r, col),
+        )
+
+    spread = [
+        [(dl, r) for dl in range(2**k) for r in range(0, n_row, 2) if dl or r]
+        for k in range(levels)
+    ]
+    others = [
+        [(dl, dr) for dl in range(2**k) for dr in range(n_row) if dl or dr] for k in range(levels)
+    ]
+
+    def leads(k):
+        return (lax.rem(lvl, 2**k) == 0) & (row == 0)
+
+    def own_piv_copy(k):
+        return pltpu.make_async_copy(
+            init_ref.at[:, pl.ds(offsets[k], tile)], piv_tile(k, 0), own_piv.at[k]
+        )
+
+    def own_rows_copy(k):
+        return pltpu.make_async_copy(
+            init_ref.at[:, pl.ds(offsets[k], tile)], rows_ref.at[k, :, tiles(col)], own_rows.at[k]
+        )
+
+    def own_cols_copy(k):
+        inner = lax.rem(lvl, 2**k)
+        return pltpu.make_async_copy(
+            rows_ref.at[k, tiles(col), :],
+            cols_refs[k].at[tiles(inner * n_row + row), :],
+            own_cols.at[k],
+        )
+
+    first_core = lax.rem(row, 2) == 0
+    for k in range(levels):
+
+        @pl.when(leads(k))
+        def _(k=k):
+            own_piv_copy(k).start()
+
+    for k in range(levels):
+
+        @pl.when(leads(k))
+        def _(k=k):
+            own_piv_copy(k).wait()
+            for slot, (dl, r) in enumerate(spread[k]):
+                spread_copy(k, slot, dl, r).start()
+
+    for k in range(levels):
+        own_rows_copy(k).start()
+        for step in range(1, n_col):
+            row_copy(k, step, 0).start()
+
+    @pl.when(first_core)
+    def _():
+        for k in range(levels):
+
+            @pl.when(~leads(k))
+            def _(k=k):
+                spread_copy(k, 0, 0, row).wait_recv()
+
+            for step in range(1, n_col):
+                line_copy(k, step).start()
+            core_copy(k, 0).start()
+        for k in range(levels):
+            for step in range(1, n_col):
+                line_arrival(k, step).wait_recv()
+                core_copy(k, step).start()
+
+    @pl.when(~first_core)
+    def _():
+        for k in range(levels):
+            for step in range(n_col):
+                core_copy(k, step).wait_recv()
+
+    for k in range(levels):
+        own_rows_copy(k).wait()
+        for step in range(1, n_col):
+            row_arrival(k, step, 0).wait_recv()
+        own_cols_copy(k).start()
+        for dl, dr in others[k]:
+            col_copy(k, dl, dr).start()
+    for k in range(levels):
+        for slot in range(1, n_col):
+            for step in range(1, n_col):
+                row_copy(k, step, slot).start()
+
+    at_row = lax.broadcasted_iota(jnp.int32, (pivots, pivots), 0) // tile
+    at_column = lax.broadcasted_iota(jnp.int32, (pivots, pivots), 1) // tile
+    for k in range(levels):
+        near = jnp.abs(lab_row_ref[k] - lab_col_ref[k]) <= 1
+        inv_ref[k] = jnp.where(near | (at_row == at_column), piv[k], 0.0)
+    eliminate(inv_ref, levels, pivots, tile)
+
+    for k in range(levels):
+        own_cols_copy(k).wait()
+        for step in range(1, n_col):
+            row_copy(k, step, 0).wait_send()
+            for slot in range(1, n_col):
+                row_copy(k, step, slot).wait_send()
+                row_arrival(k, step, slot).wait_recv()
+        for dl, dr in others[k]:
+            col_copy(k, dl, dr).wait_send()
+            col_arrival(k, dl, dr).wait_recv()
+
+        @pl.when(leads(k))
+        def _(k=k):
+            for slot, (dl, r) in enumerate(spread[k]):
+                spread_copy(k, slot, dl, r).wait_send()
+
+        @pl.when(first_core)
+        def _(k=k):
+            for step in range(n_col):
+                core_copy(k, step).wait_send()
+                if step:
+                    line_copy(k, step).wait_send()
+
+
+def gather_and_invert(initials, labels, sizes):
+    n_level, n_row, n_col, levels, tile = sizes
+    pivots = n_col * tile
+    dma = pltpu.SemaphoreType.DMA
+    square = jax.ShapeDtypeStruct((levels, pivots, pivots), jnp.float32)
+    widths = [2**k * n_row * tile for k in range(levels)]
+    results = pl.pallas_call(
+        lambda *refs: gather_kernel(sizes, *refs),
+        out_shape=[square, square]
+        + [jax.ShapeDtypeStruct((width, pivots), jnp.float32) for width in widths],
+        in_specs=[
+            pl.BlockSpec(memory_space=pl.ANY),
+            pl.BlockSpec(memory_space=pltpu.VMEM),
+            pl.BlockSpec(memory_space=pltpu.VMEM),
+        ],
+        out_specs=[pl.BlockSpec(memory_space=pltpu.VMEM)]
+        + [pl.BlockSpec(memory_space=pl.ANY)] * (levels + 1),
+        scratch_shapes=[
+            pltpu.VMEM((levels, pivots, pivots), jnp.float32),
+            dma((levels, n_level * n_row)),
+            dma((levels,)),
+            dma((levels, n_col)),
+            dma((levels, n_col)),
+            dma((levels, n_col)),
+            dma((levels, n_col)),
+            dma((levels, n_col, n_col)),
+            dma((levels, n_col, n_col)),
+            dma((levels, n_level * n_row)),
+            dma((levels, n_level * n_row)),
+            dma((levels,)),
+            dma((levels,)),
+            dma((levels,)),
+        ],
+        compiler_params=pltpu.CompilerParams(
+            vmem_limit_bytes=40 * 2**20, collective_id=0, has_side_effects=True
+        ),
         cost_estimate=pl.CostEstimate(flops=60 * 10**9, bytes_accessed=4 * 2**20, transcendentals=0),
-    )(pivot_blocks)
+    )(initials, labels[:, :, None], labels[:, None, :])
+    return results[0], results[1], results[2:]
 
 
 def dot(a, b, contract):
@@ -144,43 +430,48 @@
     rows_dev = initials.shape[0]
     tile = rows_dev // n_col
     per_level = n_row * n_col
+    sizes = (n_level, n_row, n_col, levels, tile)
+    pivot_labels = jnp.stack(
+        [
+            lax.dynamic_slice_in_dim(patches[k], lvl // 2**k * 2**k * per_level, n_col)
+            for k in range(levels)
+        ]
+    )
+    inverses, rows_piv, column_rows = gather_and_invert(
+        initials[:, 0, :], jnp.repeat(pivot_labels, tile, axis=1), sizes
+    )
     offset = 0
     fronts = []
+    pivot_rows = []
+    pivot_columns = []
     for level_k in range(levels):
         group = 2**level_k
         width = group * n_row * tile
         block = initials[:, 0, offset : offset + width]
         offset = offset + width
         front_q = lvl // group
+        first_tile = front_q * per_level * group
         row_tiles = per_level * lvl + n_col * row_idx + jnp.arange(n_col)
-        col_tiles = front_q * per_level * group + n_col * jnp.arange(group * n_row) + col_idx
+        col_tiles = first_tile + n_col * jnp.arange(group * n_row) + col_idx
+        piv_tiles = first_tile + jnp.arange(n_col)
         label_rows = lax.dynamic_slice_in_dim(
             patches[level_k], per_level * lvl + n_col * row_idx, n_col
         )
-        label_cols = pick_column(
-            patches[level_k], front_q * per_level * group, group * n_row, n_col, col_idx
-        )
-        coupled = (jnp.abs(label_rows[:, None] - label_cols[None, :]) <= 1) | (
-            row_tiles[:, None] == col_tiles[None, :]
-        )
-        cells = jnp.repeat(jnp.repeat(coupled, tile, axis=0), tile, axis=1)
-        fronts.append(jnp.where(cells, block, 0.0))
-
-    pivot_cols = jnp.stack([front[:, :tile] for front in fronts], axis=0)
-    rows_piv = lax.all_gather(pivot_cols, "col", axis=2, tiled=True)
-    piece = lax.dynamic_slice_in_dim(rows_piv, col_idx * tile, tile, 1)
-    gathered = lax.all_gather(piece, ("level", "row"), axis=1, tiled=True)
-    column_rows = []
-    for level_k in range(levels):
-        group = 2**level_k
-        column_rows.append(
-            lax.dynamic_slice_in_dim(
-                gathered[level_k], lvl // group * group * n_row * tile, group * n_row * tile, 0
+        label_cols = pick_column(patches[level_k], first_tile, group * n_row, n_col, col_idx)
+
+        def masked(value, labels_a, tiles_a, labels_b, tiles_b):
+            coupled = (jnp.abs(labels_a[:, None] - labels_b[None, :]) <= 1) | (
+                tiles_a[:, None] == tiles_b[None, :]
             )
-        )
-    heads = jnp.stack([rows[:tile] for rows in column_rows], axis=0)
-    pivot_blocks = lax.all_gather(heads, "col", axis=1, tiled=True)
-    inverses = invert(pivot_blocks)
+            cells = jnp.repeat(jnp.repeat(coupled, tile, axis=0), tile, axis=1)
+            return jnp.where(cells, value, 0.0)
+
+        label_piv = pivot_labels[level_k]
+        fronts.append(masked(block, label_rows, row_tiles, label_cols, col_tiles))
+        pivot_rows.append(masked(rows_piv[level_k], label_rows, row_tiles, label_piv, piv_tiles))
+        pivot_columns.append(
+            masked(column_rows[level_k], label_cols, col_tiles, label_piv, piv_tiles)
+        )
 
     update = None
     panel_list = []
@@ -189,8 +480,8 @@
         width = group * n_row * tile
         local_level = lvl % group
         front = fronts[level_k]
-        panel_rows = dot(rows_piv[level_k], inverses[level_k], ((1,), (1,)))
-        panel_cols = dot(inverses[level_k], column_rows[level_k], ((1,), (1,)))
+        panel_rows = dot(pivot_rows[level_k], inverses[level_k], ((1,), (1,)))
+        panel_cols = dot(inverses[level_k], pivot_columns[level_k], ((1,), (1,)))
         schur = front - dot(panel_rows, panel_cols, ((1,), (0,)))
         if level_k > 0:
             child = group // 2

time: 250 us -> 150 us (0.60)
  waiting for transfers between devices: 147 us -> 10.2 us
  Pallas kernels: 41.6 us -> 81.8 us
  between operations: 14 us -> 0.97 us
  local copies, waits for them, and re-layouts: 22.5 us -> 29.2 us
    all_gather x3 -> x0, waiting for transfers between devices: 130 us -> none  [the longest x1 49 us: local(): rows_piv = lax.all_gather(pivot_cols, 'col', axis=2, tiled=True)]
    pallas_call x1, Pallas kernels: 41.6 us -> 81.8 us  [gather_and_invert(): pl.pallas_call(lambda *refs: gather_kernel(sizes, *refs), out_shape=[squa...]
    slice x2 -> x4, local copies, waits for them, and re-layouts: 7.28 us -> 0.02 us  [local(): block = initials[:, 0, offset:offset + width]]
    ppermute x1, waiting for transfers between devices: 17 us -> 10.2 us  [from_partner(): return lax.ppermute(value, axis, pairs)]
    broadcast_in_dim x4 -> x11, local copies, waits for them, and re-layouts: 3.26 us -> 8.42 us  [the longest x10 8.35 us: masked(): cells = jnp.repeat(jnp.repeat(coupled, tile, axis=0), tile, axis=1)]
    unnamed x15 -> x18, local copies, waits for them, and re-layouts: 6.4 us -> 10.6 us
    squeeze x0 -> x2, local copies, waits for them, and re-layouts: none -> 4.13 us  [local(): rows_piv[level_k]]
  transfers between devices with their start and end apart: 4 -> 1, of which waited for: 4 -> 1; matrix products, arithmetic and copies ran while one was open for 3% -> 10% of each run, Pallas kernels for 0% -> 0%
where the time goes in v2:
time: 150 us; the launch traced here: 148 us
  Pallas kernels  81.8 us (55%)
  local copies, waits for them, and re-layouts  29.2 us (19%)
  matrix products  17.2 us (11%)
  waiting for transfers between devices  10.2 us (7%)
  other arithmetic  7.96 us (5%)
    pallas_call x1, Pallas kernels, gather_and_invert(): pl.pallas_call(lambda *refs: gather_kernel(sizes, *refs), out_shape=[squa...  81.8 us
    dot_general x6, matrix products, dot(): lax.dot_general(a, b, (contract, ((), ())), precision=HIGHEST, preferred_...  17.2 us
    unnamed x18, local copies, waits for them, and re-layouts  10.6 us
    ppermute x1, waiting for transfers between devices, from_partner(): return lax.ppermute(value, axis, pairs)  10.2 us
    broadcast_in_dim x10, local copies, waits for them, and re-layouts, masked(): cells = jnp.repeat(jnp.repeat(coupled, tile, axis=0), tile, axis=1)  8.35 us
    select_n x2, other arithmetic, masked(): return jnp.where(cells, value, 0.0)  4.84 us
    squeeze x2, local copies, waits for them, and re-layouts, local(): rows_piv[level_k]  4.13 us
  transfers between devices with their start and end apart: 1, of which 1 were waited for; matrix products, arithmetic and copies ran while one was open for 10% of the time, Pallas kernels for 0%

profile of v2, /device:TPU:0, one launch (start us, length us, event | category | flops | bytes accessed | tf_op | source)
XLA Modules:
  0.0 147.9 jit_solution(9295146003548886597)
XLA Ops:
  0.7 0.8 slice_reduce_fusion
  1.5 0.8 fusion.43
  2.3 0.1 reshape.196
  2.5 0.2 select_reduce_fusion.1
  2.9 3.8 %copy.55 = f32[512,1,1536]{2,0,1:T(8,128)} copy(f32[512,1,1536]{2,1,0:T(1,128)} %param.3) | data formatting | bytes 6291456
  6.8 1.1 broadcast_in_dim_reshape.22.refs_1_
  7.9 1.9 %copy-done = f32[512,1,1536]{2,0,1:T(8,128)S(1)} copy-done((f32[512,1,1536]{2,0,1:T(8,128)S(1)}, f32[512,1,1536]{2,0,1:T(8,128)}, u32[]{:S(2)}) %copy-start) | copy-done | bytes 3145752
  9.8 1.0 copy-done.3
  10.9 81.8 %shard_map.50 = (f32[2,512,512]{2,1,0:T(8,128)S(1)}, f32[2,512,512]{2,1,0:T(8,128)S(1)}, f32[512,512]{1,0:T(8,128)S(1)}, f32[1024,512]{1,0:T(8,128)S(1)}) custom-call(f32[512,1536]{1,0:T(8,128)S(1)} %bitcast.90, s32[2,512,1]{2,1,0:T(8,128)S(1)} %copy-done.3, s32[2,1,512]{2,1,0:T(1,128)S(1)} %bitcast.91), custom_call_target="tpu_custom_call" | custom-call | flops 60000002048 | bytes 4194304 | tf_op jit(solution)/shard_map/pallas_call | solution.py:381
  92.7 1.6 %fusion.46 = (f32[1,512,512]{2,1,0:T(8,128)}, f32[1,512,512]{2,1,0:T(8,128)}) fusion(f32[2,512,512]{2,1,0:T(8,128)S(1)} %get-tuple-element.6), kind=kLoop, calls=%fused_computation.99 | loop fusion | bytes 4194304 | tf_op jit(solution)/shard_map/slice | solution.py:471
  94.3 0.4 copy-done.1
  94.7 2.6 %squeeze.15 = f32[512,4,128]{2,1,0:T(4,128)} reshape(f32[1,512,512]{2,1,0:T(8,128)} %get-tuple-element.19) | data formatting | bytes 2097152 | tf_op jit(solution)/shard_map/squeeze | solution.py:471
  97.5 3.2 %broadcast_select_fusion.1 = f32[512,4,128]{2,1,0:T(4,128)S(1)} fusion(f32[512,4,128]{2,1,0:T(4,128)} %squeeze.15, pred[512,4]{1,0:T(8,128)(4,1)S(1)} %bitcast.99), kind=kLoop, calls=%fused_computation.42 | loop fusion | flops 262144 | bytes 2099200 | tf_op jit(solution)/shard_map/jit(_where)/select_n | solution.py:467
  100.8 1.9 %fusion.13 = f32[512,512]{1,0:T(8,128)S(1)} fusion(f32[64,8,4,128]{3,2,1,0:T(4,128)S(1)} %bitcast.92, f32[2,512,512]{2,1,0:T(8,128)S(1)} %get-tuple-element.7), kind=kOutput, calls=%fused_computation.17 | convolution fusion | flops 1610612736 | bytes 3145728 | tf_op jit(solution)/shard_map/dot_general | solution.py:417
  102.7 1.6 %broadcast_in_dim.177 = pred[512,4,128]{2,1,0:T(4,128)(4,1)S(1)} broadcast(pred[512,4]{1,0:T(8,128)(4,1)S(1)} %bitcast.101), dimensions={0,1} | broadcast | bytes 264192 | tf_op jit(solution)/shard_map/broadcast_in_dim | solution.py:466
  104.3 1.9 %fusion.19 = f32[512,512]{1,0:T(8,128)S(1)} fusion(f32[512,512]{1,0:T(8,128)S(1)} %get-tuple-element.9, pred[64,8,4,128]{3,2,1,0:T(4,128)(4,1)S(1)} %bitcast.97, f32[2,512,512]{2,1,0:T(8,128)S(1)} %get-tuple-element.7), kind=kOutput, calls=%fused_computation.24 | convolution fusion | flops 1610874880 | bytes 3407872 | tf_op jit(solution)/shard_map/dot_general | solution.py:417
  106.3 1.6 %broadcast_in_dim.174 = pred[512,4,128]{2,1,0:T(4,128)(4,1)S(1)} broadcast(pred[512,4]{1,0:T(8,128)(4,1)S(1)} %bitcast.102), dimensions={0,1} | broadcast | bytes 264192 | tf_op jit(solution)/shard_map/broadcast_in_dim | solution.py:466
  107.9 3.9 %and_select_fusion.3 = (f32[512,512]{1,0:T(8,128)}, f32[512,512]{1,0:T(8,128)}, f32[512,512]{1,0:T(8,128)}) fusion(pred[512]{0:T(512)(128)(4,1)S(1)} %bitcast_not_fusion.1, pred[512]{0:T(512)(128)(4,1)S(1)} %broadcast_bitcast_fusion.3, pred[512]{0:T(512)(128)(4,1)S(1)} %broadcast_bitcast_fusion.2, f32[512,512]{1,0:T(8,128)S(1)} %fusion.13, ...), kind=kOutput, calls=%fused_computation.34 | convolution fusion | flops 1612447744 | bytes 6555648 | tf_op jit(solution)/shard_map/dot_general | solution.py:417
  111.7 0.6 collective-permute-start
  112.5 0.1 select_reduce_fusion
  112.6 1.6 %squeeze.33 = f32[512,4,128]{2,1,0:T(4,128)S(1)} reshape(f32[1,512,512]{2,1,0:T(8,128)} %get-tuple-element.20) | data formatting | bytes 2097152 | tf_op jit(solution)/shard_map/squeeze | solution.py:471
  114.2 1.6 %broadcast_select_fusion = f32[512,4,128]{2,1,0:T(4,128)S(1)} fusion(f32[512,4,128]{2,1,0:T(4,128)S(1)} %squeeze.33, pred[512,4]{1,0:T(8,128)(4,1)S(1)} %bitcast.100), kind=kLoop, calls=%fused_computation.41 | loop fusion | flops 262144 | bytes 2099200 | tf_op jit(solution)/shard_map/jit(_where)/select_n | solution.py:467
  115.9 1.9 %fusion.10 = f32[512,512]{1,0:T(8,128)S(1)} fusion(f32[64,8,4,128]{3,2,1,0:T(4,128)S(1)} %bitcast.93, f32[2,512,512]{2,1,0:T(8,128)S(1)} %get-tuple-element.7), kind=kOutput, calls=%fused_computation.14 | convolution fusion | flops 1610612736 | bytes 3145728 | tf_op jit(solution)/shard_map/dot_general | solution.py:417
  117.8 1.0 dynamic-slice_bitcast_fusion.1
  118.8 0.8 pad_maximum_fusion
  119.9 3.4 %broadcast_in_dim.166 = pred[1024,4,128]{2,1,0:T(4,128)(4,1)S(1)} broadcast(pred[1024,4]{1,0:T(8,128)(4,1)S(1)} %bitcast.98), dimensions={0,1} | broadcast | bytes 528384 | tf_op jit(solution)/shard_map/broadcast_in_dim | solution.py:466
  123.3 3.6 %fusion.5 = f32[512,1024]{1,0:T(8,128)S(1)} fusion(f32[1024,512]{1,0:T(8,128)S(1)} %copy-done.2, pred[128,8,4,128]{3,2,1,0:T(4,128)(4,1)S(1)} %bitcast.95, f32[2,512,512]{2,1,0:T(8,128)S(1)} %get-tuple-element.7), kind=kOutput, calls=%fused_computation.8 | convolution fusion | flops 3221749760 | bytes 5767168 | tf_op jit(solution)/shard_map/dot_general | solution.py:417
  127.0 10.2 %collective-permute-done = f32[512,512]{1,0:T(8,128)} collective-permute-done((f32[512,512]{1,0:T(8,128)}, f32[512,512]{1,0:T(8,128)}, u32[]{:S(2)}, u32[]{:S(2)}) %collective-permute-start) | collective-permute-done | bytes 1048608 | tf_op jit(solution)/shard_map/ppermute | solution.py:16
  137.2 1.5 %and_select_fusion.1 = (f32[512,512]{1,0:T(8,128)S(1)}, f32[512,512]{1,0:T(8,128)S(1)}) fusion(f32[512,512]{1,0:T(8,128)} %collective-permute-done, pred[512]{0:T(512)(128)(4,1)S(1)} %bitcast_not_fusion, pred[512]{0:T(512)(128)(4,1)S(1)} %broadcast_bitcast_fusion.1, pred[512]{0:T(512)(128)(4,1)S(1)} %broadcast_bitcast_fusion), kind=kLoop, calls=%fused_computation.32 | loop fusion | flops 1048576 | bytes 3147264 | tf_op jit(solution)/shard_map/jit(_where)/select_n | solution.py:28
  138.7 1.6 %broadcast_in_dim.163 = pred[512,8,128]{2,1,0:T(8,128)(4,1)S(1)} broadcast(pred[512,8]{1,0:T(8,128)(4,1)S(1)} %bitcast.103), dimensions={0,1} | broadcast | bytes 528384 | tf_op jit(solution)/shard_map/broadcast_in_dim | solution.py:466
  140.4 4.1 %fusion.2 = f32[512,1,1024]{2,0,1:T(8,128)S(1)} fusion(f32[512,512]{1,0:T(8,128)S(1)} %copy-done.6, f32[512,512]{1,0:T(8,128)S(1)} %copy-done.5, f32[512,512]{1,0:T(8,128)S(1)} %get-tuple-element.22, f32[512,512]{1,0:T(8,128)S(1)} %get-tuple-element.21, f32[512,1,1024]{2,1,0:T(1,128)S(1)} %slice-done.1, pred[64,8,8,128]{3,2,1,0:T(8,128)(4,1)S(1)} %bitcast.94, ...), kind=kOutput, calls=%fused_computation.4 | convolution fusion | flops 3224895488 | bytes 12059648 | tf_op jit(solution)/shard_map/dot_general | solution.py:417
  144.4 3.5 %copy.13 = f32[512,1,1024]{2,1,0:T(1,128)} copy(f32[512,1,1024]{2,0,1:T(8,128)S(1)} %fusion.2) | data formatting | bytes 4194304
  (48 shorter events, 1.4 us)
Async XLA Ops:
  7.9 1.9 %copy-start = (f32[512,1,1536]{2,0,1:T(8,128)S(1)}, f32[512,1,1536]{2,0,1:T(8,128)}, u32[]{:S(2)}) copy-start(f32[512,1,1536]{2,0,1:T(8,128)} %copy.55) | copy-start | bytes 9437188
  9.8 1.0 copy-start.3
  92.7 2.0 %copy-start.1 = (f32[1024,512]{1,0:T(8,128)}, f32[1024,512]{1,0:T(8,128)S(1)}, u32[]{:S(2)}) copy-start(f32[1024,512]{1,0:T(8,128)S(1)} %get-tuple-element.8) | copy-start | bytes 6291460
  94.7 2.6 %copy-start.7 = (s32[1,32]{1,0:T(1,128)S(1)}, s32[1,32]{1,0:T(1,128)}, u32[]{:S(2)}) copy-start(s32[1,32]{1,0:T(1,128)} %param.5) | copy-start | bytes 388
  102.6 5.2 %copy-start.4 = (f32[512,512]{1,0:T(8,128)}, f32[512,512]{1,0:T(8,128)S(1)}, u32[]{:S(2)}) copy-start(f32[512,512]{1,0:T(8,128)S(1)} %fusion.13) | copy-start | bytes 3145732
  102.6 5.2 %slice-start = ((f32[512,1,1536]{2,1,0:T(1,128)}), f32[512,1,512]{2,1,0:T(1,128)S(1)}, s32[]{:S(2)}) async-start(f32[512,1,1536]{2,1,0:T(1,128)} %param.3), calls=%async_computation | async-start | bytes 2097152 | tf_op jit(solution)/shard_map/slice | solution.py:450
  111.7 25.4 %collective-permute-start = (f32[512,512]{1,0:T(8,128)}, f32[512,512]{1,0:T(8,128)}, u32[]{:S(2)}, u32[]{:S(2)}) collective-permute-start(f32[512,512]{1,0:T(8,128)} %get-tuple-element.38), channel_id=1, source_target_pairs={{0,16},{16,0},{1,17},{17,1},{2,18},{18,2},{3,19},{19,3},{4,20},{20... | collective-permute-start | bytes 3145736 | tf_op jit(solution)/shard_map/ppermute | solution.py:16
  119.6 3.7 %copy-start.2 = (f32[1024,512]{1,0:T(8,128)S(1)}, f32[1024,512]{1,0:T(8,128)}, u32[]{:S(2)}) copy-start(f32[1024,512]{1,0:T(8,128)} %copy-done.1) | copy-start | bytes 6291460
  123.3 17.0 %copy-start.6 = (f32[512,512]{1,0:T(8,128)S(1)}, f32[512,512]{1,0:T(8,128)}, u32[]{:S(2)}) copy-start(f32[512,512]{1,0:T(8,128)} %get-tuple-element.24) | copy-start | bytes 3145732
  127.0 13.4 %slice-start.1 = ((f32[512,1,1536]{2,1,0:T(1,128)}), f32[512,1,1024]{2,1,0:T(1,128)S(1)}, s32[]{:S(2)}) async-start(f32[512,1,1536]{2,1,0:T(1,128)} %param.3), calls=%async_computation.1 | async-start | bytes 4194304 | tf_op jit(solution)/shard_map/slice | solution.py:450
  127.0 13.4 %copy-start.5 = (f32[512,512]{1,0:T(8,128)S(1)}, f32[512,512]{1,0:T(8,128)}, u32[]{:S(2)}) copy-start(f32[512,512]{1,0:T(8,128)} %get-tuple-element.23) | copy-start | bytes 3145732

commit v3 on v2

--- a/solution.py
+++ b/solution.py
@@ -81,15 +81,19 @@
     return [jnp.concatenate(done, axis=0) for done in results]
 
 
-def eliminate(state, fronts, pivots, tile):
+def eliminate(state, fronts, pivots, tile, block_row, between):
     col = lax.broadcasted_iota(jnp.int32, (tile, pivots), 1)
     big_col = lax.broadcasted_iota(jnp.int32, (pivots, pivots), 1)
     big_row = lax.broadcasted_iota(jnp.int32, (pivots, pivots), 0)
 
+    state[...] = jnp.zeros_like(state)
+
     def body(b, carry):
         start = pl.multiple_of(b * tile, tile)
         here = pl.ds(start, tile)
+        block_row(b)
         diag = inverse_factor([state[f, here, here] for f in range(fronts)])
+        between(b)
         for f in range(fronts):
             row = jnp.dot(
                 diag[f], state[f, here, :], precision=HIGHEST, preferred_element_type=jnp.float32
@@ -193,38 +197,42 @@
             at_col(step),
         )
 
-    def piv_tile(k, step):
-        return piv.at[k, :, tiles(lax.rem(col + n_col - step, n_col))]
-
-    def line_copy(k, step):
-        return remote(
-            piv_tile(k, 0), piv_tile(k, 0), line_send.at[k, step], line_recv.at[k, step], at_col(step)
-        )
-
-    def line_arrival(k, step):
-        return remote(
-            piv_tile(k, step),
-            piv_tile(k, step),
-            line_send.at[k, step],
-            line_recv.at[k, step],
+    def piv_tile(k, step, r):
+        return piv.at[k, tiles(r), tiles(lax.rem(col + n_col - step, n_col))]
+
+    def line_copy(k, step, r):
+        return remote(
+            piv_tile(k, 0, r),
+            piv_tile(k, 0, r),
+            line_send.at[k, step, r],
+            line_recv.at[k, step, r],
             at_col(step),
         )
 
-    def core_copy(k, step):
-        return remote(
-            piv_tile(k, step),
-            piv_tile(k, step),
-            core_send.at[k, step],
-            core_recv.at[k, step],
+    def line_arrival(k, step, r):
+        return remote(
+            piv_tile(k, step, r),
+            piv_tile(k, step, r),
+            line_send.at[k, step, r],
+            line_recv.at[k, step, r],
+            at_col(step),
+        )
+
+    def core_copy(k, step, r):
+        return remote(
+            piv_tile(k, step, r),
+            piv_tile(k, step, r),
+            core_send.at[k, step, r],
+            core_recv.at[k, step, r],
             (lvl, row // 2 * 2 + 1 - lax.rem(row, 2), col),
         )
 
-    def spread_copy(k, slot, dl, to_row):
-        return remote(
-            piv_tile(k, 0),
-            piv_tile(k, 0),
-            spread_send.at[k, slot],
-            spread_recv.at[k],
+    def spread_copy(k, slot, dl, to_row, r):
+        return remote(
+            piv_tile(k, 0, r),
+            piv_tile(k, 0, r),
+            spread_send.at[k, slot, r],
+            spread_recv.at[k, r],
             (lax.rem(lvl + dl, n_level), to_row, col),
         )
 
@@ -271,7 +279,7 @@
 
     def own_piv_copy(k):
         return pltpu.make_async_copy(
-            init_ref.at[:, pl.ds(offsets[k], tile)], piv_tile(k, 0), own_piv.at[k]
+            init_ref.at[:, pl.ds(offsets[k], tile)], piv.at[k, :, tiles(col)], own_piv.at[k]
         )
 
     def own_rows_copy(k):
@@ -299,54 +307,81 @@
         @pl.when(leads(k))
         def _(k=k):
             own_piv_copy(k).wait()
-            for slot, (dl, r) in enumerate(spread[k]):
-                spread_copy(k, slot, dl, r).start()
+
+    for r in range(n_col):
+        for k in range(levels):
+
+            @pl.when(leads(k))
+            def _(k=k, r=r):
+                for slot, (dl, to_row) in enumerate(spread[k]):
+                    spread_copy(k, slot, dl, to_row, r).start()
 
     for k in range(levels):
         own_rows_copy(k).start()
+
+    @pl.when(first_core)
+    def _():
+        for r in range(n_col):
+            for k in range(levels):
+
+                @pl.when(~leads(k))
+                def _(k=k, r=r):
+                    spread_copy(k, 0, 0, row, r).wait_recv()
+
+                for step in range(1, n_col):
+                    line_copy(k, step, r).start()
+                core_copy(k, 0, r).start()
+
+    for k in range(levels):
         for step in range(1, n_col):
             row_copy(k, step, 0).start()
 
-    @pl.when(first_core)
-    def _():
+    def advance(r):
+        @pl.when(first_core)
+        def _():
+            for k in range(levels):
+                for step in range(1, n_col):
+                    line_arrival(k, step, r).wait_recv()
+                    core_copy(k, step, r).start()
+
+    wide_col = lax.broadcasted_iota(jnp.int32, (tile, pivots), 1)
+
+    def block_row(b):
+        @pl.when(~first_core)
+        def _():
+            for k in range(levels):
+                for step in range(n_col):
+                    core_copy(k, step, b).wait_recv()
+
+        here = tiles(b)
+        start = b * tile
         for k in range(levels):
-
-            @pl.when(~leads(k))
-            def _(k=k):
-                spread_copy(k, 0, 0, row).wait_recv()
-
-            for step in range(1, n_col):
-                line_copy(k, step).start()
-            core_copy(k, 0).start()
-        for k in range(levels):
-            for step in range(1, n_col):
-                line_arrival(k, step).wait_recv()
-                core_copy(k, step).start()
-
-    @pl.when(~first_core)
-    def _():
-        for k in range(levels):
-            for step in range(n_col):
-                core_copy(k, step).wait_recv()
-
-    for k in range(levels):
-        own_rows_copy(k).wait()
-        for step in range(1, n_col):
-            row_arrival(k, step, 0).wait_recv()
-        own_cols_copy(k).start()
-        for dl, dr in others[k]:
-            col_copy(k, dl, dr).start()
-    for k in range(levels):
-        for slot in range(1, n_col):
-            for step in range(1, n_col):
-                row_copy(k, step, slot).start()
-
-    at_row = lax.broadcasted_iota(jnp.int32, (pivots, pivots), 0) // tile
-    at_column = lax.broadcasted_iota(jnp.int32, (pivots, pivots), 1) // tile
-    for k in range(levels):
-        near = jnp.abs(lab_row_ref[k] - lab_col_ref[k]) <= 1
-        inv_ref[k] = jnp.where(near | (at_row == at_column), piv[k], 0.0)
-    eliminate(inv_ref, levels, pivots, tile)
+            near = jnp.abs(lab_row_ref[k, here, :] - lab_col_ref[k]) <= 1
+            same = wide_col < start + tile
+            keep = (near | same) & (wide_col >= start)
+            inv_ref[k, here, :] = inv_ref[k, here, :] + jnp.where(keep, piv[k, here, :], 0.0)
+
+    def between(b):
+        @pl.when(b < n_col - 1)
+        def _():
+            advance(b + 1)
+
+        @pl.when(b == 0)
+        def _():
+            for k in range(levels):
+                own_rows_copy(k).wait()
+                for step in range(1, n_col):
+                    row_arrival(k, step, 0).wait_recv()
+                own_cols_copy(k).start()
+                for dl, dr in others[k]:
+                    col_copy(k, dl, dr).start()
+            for k in range(levels):
+                for slot in range(1, n_col):
+                    for step in range(1, n_col):
+                        row_copy(k, step, slot).start()
+
+    advance(0)
+    eliminate(inv_ref, levels, pivots, tile, block_row, between)
 
     for k in range(levels):
         own_cols_copy(k).wait()
@@ -361,15 +396,17 @@
 
         @pl.when(leads(k))
         def _(k=k):
-            for slot, (dl, r) in enumerate(spread[k]):
-                spread_copy(k, slot, dl, r).wait_send()
+            for slot, (dl, to_row) in enumerate(spread[k]):
+                for r in range(n_col):
+                    spread_copy(k, slot, dl, to_row, r).wait_send()
 
         @pl.when(first_core)
         def _(k=k):
             for step in range(n_col):
-                core_copy(k, step).wait_send()
-                if step:
-                    line_copy(k, step).wait_send()
+                for r in range(n_col):
+                    core_copy(k, step, r).wait_send()
+                    if step:
+                        line_copy(k, step, r).wait_send()
 
 
 def gather_and_invert(initials, labels, sizes):
@@ -391,12 +428,12 @@
         + [pl.BlockSpec(memory_space=pl.ANY)] * (levels + 1),
         scratch_shapes=[
             pltpu.VMEM((levels, pivots, pivots), jnp.float32),
-            dma((levels, n_level * n_row)),
-            dma((levels,)),
+            dma((levels, n_level * n_row, n_col)),
             dma((levels, n_col)),
-            dma((levels, n_col)),
-            dma((levels, n_col)),
-            dma((levels, n_col)),
+            dma((levels, n_col, n_col)),
+            dma((levels, n_col, n_col)),
+            dma((levels, n_col, n_col)),
+            dma((levels, n_col, n_col)),
             dma((levels, n_col, n_col)),
             dma((levels, n_col, n_col)),
             dma((levels, n_level * n_row)),
@@ -411,6 +448,78 @@
         cost_estimate=pl.CostEstimate(flops=60 * 10**9, bytes_accessed=4 * 2**20, transcendentals=0),
     )(initials, labels[:, :, None], labels[:, None, :])
     return results[0], results[1], results[2:]
+
+
+def schur_kernel(k, sizes, patches_ref, inv_ref, rows_ref, cols_ref, front_ref, panel_ref, out_ref, panel):
+    n_row, n_col, tile = sizes
+    group = 2**k
+    j = pl.program_id(0)
+    lvl = lax.axis_index("level")
+    row = lax.axis_index("row")
+    col = lax.axis_index("col")
+    per_level = n_row * n_col
+    first = lvl // group * group * per_level
+    row_tiles = [per_level * lvl + n_col * row + t for t in range(n_col)]
+    col_tiles = [first + n_col * (j * n_row + t) + col for t in range(n_row)]
+    piv_tiles = [first + t for t in range(n_col)]
+
+    def masked(ref, tiles_a, tiles_b):
+        labels_a = [patches_ref[k, t] for t in tiles_a]
+        labels_b = [patches_ref[k, t] for t in tiles_b]
+        strips = []
+        for a, tile_a in enumerate(tiles_a):
+            parts = []
+            for b, tile_b in enumerate(tiles_b):
+                keep = (jnp.abs(labels_a[a] - labels_b[b]) <= 1) | (tile_a == tile_b)
+                block = ref[a * tile : (a + 1) * tile, b * tile : (b + 1) * tile]
+                parts.append(jnp.where(keep, block, 0.0))
+            strips.append(jnp.concatenate(parts, axis=1))
+        return jnp.concatenate(strips, axis=0)
+
+    @pl.when(j == 0)
+    def _():
+        panel[...] = dot(masked(rows_ref, row_tiles, piv_tiles), inv_ref[...], ((1,), (1,)))
+        panel_ref[...] = panel[:, pl.ds(pl.multiple_of(col * tile, tile), tile)]
+
+    across = dot(inv_ref[...], masked(cols_ref, col_tiles, piv_tiles), ((1,), (1,)))
+    schur = masked(front_ref, row_tiles, col_tiles) - dot(panel[...], across, ((1,), (0,)))
+    at_col = lax.broadcasted_iota(jnp.int32, schur.shape, 1)
+    lead = (lax.rem(lvl, group) == 0) & (row == 0)
+    drop = (at_col < jnp.where(j == 0, tile, 0)) | (at_col < jnp.where(lead, n_row * tile, 0))
+    out_ref[...] = jnp.where(drop, 0.0, schur)
+
+
+def panel_and_schur(k, sizes, patches, inverses, rows_piv, columns, flat):
+    n_row, n_col, tile = sizes
+    group = 2**k
+    high = n_col * tile
+    wide = n_row * tile
+    return pl.pallas_call(
+        lambda *refs: schur_kernel(k, sizes, *refs),
+        grid=(group,),
+        out_shape=[
+            jax.ShapeDtypeStruct((high, tile), jnp.float32),
+            jax.ShapeDtypeStruct((high, group * wide), jnp.float32),
+        ],
+        in_specs=[
+            pl.BlockSpec(memory_space=pltpu.SMEM),
+            pl.BlockSpec((None, high, high), lambda j: (k, 0, 0)),
+            pl.BlockSpec((None, high, high), lambda j: (k, 0, 0)),
+            pl.BlockSpec((wide, high), lambda j: (j, 0)),
+            pl.BlockSpec((high, wide), lambda j: (0, group - 1 + j)),
+        ],
+        out_specs=[
+            pl.BlockSpec((high, tile), lambda j: (0, 0)),
+            pl.BlockSpec((high, wide), lambda j: (0, j)),
+        ],
+        scratch_shapes=[pltpu.VMEM((high, high), jnp.float32)],
+        compiler_params=pltpu.CompilerParams(vmem_limit_bytes=40 * 2**20),
+        cost_estimate=pl.CostEstimate(
+            flops=12 * (2 * group + 1) * high**3,
+            bytes_accessed=4 * (3 * group + 2) * high * high,
+            transcendentals=0,
+        ),
+    )(patches, inverses, rows_piv, columns, flat)
 
 
 def dot(a, b, contract):
@@ -437,52 +546,25 @@
             for k in range(levels)
         ]
     )
+    flat = initials[:, 0, :]
     inverses, rows_piv, column_rows = gather_and_invert(
-        initials[:, 0, :], jnp.repeat(pivot_labels, tile, axis=1), sizes
+        flat, jnp.repeat(pivot_labels, tile, axis=1), sizes
     )
-    offset = 0
-    fronts = []
-    pivot_rows = []
-    pivot_columns = []
-    for level_k in range(levels):
-        group = 2**level_k
-        width = group * n_row * tile
-        block = initials[:, 0, offset : offset + width]
-        offset = offset + width
-        front_q = lvl // group
-        first_tile = front_q * per_level * group
-        row_tiles = per_level * lvl + n_col * row_idx + jnp.arange(n_col)
-        col_tiles = first_tile + n_col * jnp.arange(group * n_row) + col_idx
-        piv_tiles = first_tile + jnp.arange(n_col)
-        label_rows = lax.dynamic_slice_in_dim(
-            patches[level_k], per_level * lvl + n_col * row_idx, n_col
-        )
-        label_cols = pick_column(patches[level_k], first_tile, group * n_row, n_col, col_idx)
-
-        def masked(value, labels_a, tiles_a, labels_b, tiles_b):
-            coupled = (jnp.abs(labels_a[:, None] - labels_b[None, :]) <= 1) | (
-                tiles_a[:, None] == tiles_b[None, :]
-            )
-            cells = jnp.repeat(jnp.repeat(coupled, tile, axis=0), tile, axis=1)
-            return jnp.where(cells, value, 0.0)
-
-        label_piv = pivot_labels[level_k]
-        fronts.append(masked(block, label_rows, row_tiles, label_cols, col_tiles))
-        pivot_rows.append(masked(rows_piv[level_k], label_rows, row_tiles, label_piv, piv_tiles))
-        pivot_columns.append(
-            masked(column_rows[level_k], label_cols, col_tiles, label_piv, piv_tiles)
-        )
-
     update = None
     panel_list = []
     for level_k in range(levels):
         group = 2**level_k
         width = group * n_row * tile
         local_level = lvl % group
-        front = fronts[level_k]
-        panel_rows = dot(pivot_rows[level_k], inverses[level_k], ((1,), (1,)))
-        panel_cols = dot(inverses[level_k], pivot_columns[level_k], ((1,), (1,)))
-        schur = front - dot(panel_rows, panel_cols, ((1,), (0,)))
+        panel, schur = panel_and_schur(
+            level_k,
+            (n_row, n_col, tile),
+            patches,
+            inverses,
+            rows_piv,
+            column_rows[level_k],
+            flat,
+        )
         if level_k > 0:
             child = group // 2
             side = lvl // child % 2
@@ -501,10 +583,11 @@
             )
             schur = schur + place_update(update, own_rows, own_cols, side, tile)
             schur = schur + place_update(partner_update, other_rows, other_cols, side, tile)
-        keep_row = ~((local_level == 0) & (row_idx == 0))
-        keep_col = jnp.arange(width) >= tile
-        update = jnp.where(keep_row & keep_col[None, :], schur, 0.0)
-        panel_list.append(lax.dynamic_slice_in_dim(panel_rows, col_idx * tile, tile, 1))
+            keep_row = ~((local_level == 0) & (row_idx == 0))
+            keep_col = jnp.arange(width) >= tile
+            schur = jnp.where(keep_row & keep_col[None, :], schur, 0.0)
+        update = schur
+        panel_list.append(panel)
     return (jnp.stack(panel_list, axis=0), update[:, None, :])
 
 

time: 150 us -> 132 us (0.88); the launches traced: 148 us -> 132 us
  Pallas kernels: 81.8 us -> 107 us
  matrix products: 17.2 us -> 0 us
  local copies, waits for them, and re-layouts: 29.2 us -> 15.1 us
  waiting for transfers between devices: 10.2 us -> 1.64 us
  other arithmetic: 7.96 us -> 5.94 us
    dot_general x6 -> x0, matrix products: 17.2 us -> none  [dot(): lax.dot_general(a, b, (contract, ((), ())), precision=HIGHEST, preferred_...]
    pallas_call x0 -> x2, Pallas kernels: none -> 17.1 us  [panel_and_schur(): pl.pallas_call(lambda *refs: schur_kernel(k, sizes, *refs), grid=(group,)...]
    ppermute x1, waiting for transfers between devices: 10.2 us -> 1.64 us  [from_partner(): return lax.ppermute(value, axis, pairs)]
    broadcast_in_dim x10 -> x0, local copies, waits for them, and re-layouts: 8.35 us -> none  [masked(): cells = jnp.repeat(jnp.repeat(coupled, tile, axis=0), tile, axis=1)]
    pallas_call x1, Pallas kernels: 81.8 us -> 90 us  [gather_and_invert(): pl.pallas_call(lambda *refs: gather_kernel(sizes, *refs), out_shape=[squa...]
    select_n x2 -> x0, other arithmetic: 4.84 us -> none  [masked(): return jnp.where(cells, value, 0.0)]
    squeeze x2 -> x0, local copies, waits for them, and re-layouts: 4.13 us -> none  [local(): rows_piv[level_k]]
    unnamed x18 -> x26, local copies, waits for them, and re-layouts: 10.6 us -> 13.4 us
  transfers between devices with their start and end apart: 1 -> 1, of which waited for: 1 -> 1; matrix products, arithmetic and copies ran while one was open for 10% -> 3% of each run, Pallas kernels for 0% -> 8%
where the time goes in v3:
time: 132 us
  Pallas kernels  107 us (81%)
  local copies, waits for them, and re-layouts  15.1 us (11%)
  other arithmetic  5.94 us (4%)
  waiting for transfers between devices  1.64 us (1%)
  starting transfers between devices  1.32 us (1%)
    pallas_call x1, Pallas kernels, gather_and_invert(): pl.pallas_call(lambda *refs: gather_kernel(sizes, *refs), out_shape=[squa...  90 us
    pallas_call x2, Pallas kernels, panel_and_schur(): pl.pallas_call(lambda *refs: schur_kernel(k, sizes, *refs), grid=(group,)...  17.1 us
    unnamed x26, local copies, waits for them, and re-layouts  13.4 us
    select_n x2, other arithmetic, place_update(): lower_part = jnp.where(row_keep[:, None] & ~col_high[None, :], update, 0.0)  3.01 us
  transfers between devices with their start and end apart: 1, of which 1 were waited for; matrix products, arithmetic and copies ran while one was open for 3% of the time, Pallas kernels for 8%

profile of v3, /device:TPU:0, one launch (start us, length us, event | category | flops | bytes accessed | tf_op | source)
XLA Modules:
  0.0 131.9 jit_solution(8253801506195330323)
XLA Ops:
  0.7 2.1 %copy.10 = f32[512,1,1536]{2,0,1:T(8,128)S(1)} copy(f32[512,1,1536]{2,1,0:T(1,128)} %param.3) | data formatting | bytes 6291456
  2.8 0.1 constant_dynamic-slice_fusion.4
  2.9 0.1 broadcast_in_dim.56
  3.0 1.1 broadcast_in_dim_reshape.22.refs_1_
  4.1 1.0 copy-done.2
  5.1 90.0 %shard_map.50 = (f32[2,512,512]{2,1,0:T(8,128)S(1)}, f32[2,512,512]{2,1,0:T(8,128)S(1)}, f32[512,512]{1,0:T(8,128)S(1)}, f32[1024,512]{1,0:T(8,128)S(1)}) custom-call(f32[512,1536]{1,0:T(8,128)S(1)} %bitcast.22, s32[2,512,1]{2,1,0:T(8,128)S(1)} %copy-done.2, s32[2,1,512]{2,1,0:T(1,128)S(1)} %bitcast.27), custom_call_target="tpu_custom_call" | custom-call | flops 60000002048 | bytes 4194304 | tf_op jit(solution)/shard_map/pallas_call | solution.py:418
  95.1 0.0 copy-start.5
  95.2 6.8 %shard_map.51 = (f32[512,128]{1,0:T(8,128)S(1)}, f32[512,512]{1,0:T(8,128)}) custom-call(s32[2,32]{1,0:T(2,128)S(1)} %copy-done.4, f32[2,512,512]{2,1,0:T(8,128)S(1)} %get-tuple-element.10.refs_1_, f32[2,512,512]{2,1,0:T(8,128)S(1)} %get-tuple-element.11.refs_2_, f32[512,512]{1,0:T(8,128)S(1)} %get-tuple-element.12.refs_3_, f32[512,1536]{1,0:T(8,128)S(1)} %bitcast.23), custom_call_target="tpu_custom_call" | custom-call | flops 4831838208 | bytes 5242880 | tf_op jit(solution)/shard_map/pallas_call | solution.py:497
  101.9 1.3 %collective-permute-start = (f32[512,512]{1,0:T(8,128)}, f32[512,512]{1,0:T(8,128)}, u32[]{:S(2)}, u32[]{:S(2)}) collective-permute-start(f32[512,512]{1,0:T(8,128)} %get-tuple-element.17), channel_id=1, source_target_pairs={{0,16},{16,0},{1,17},{17,1},{2,18},{18,2},{3,19},{19,3},{4,20},{20... | collective-permute-start | bytes 3145736 | tf_op jit(solution)/shard_map/ppermute | solution.py:16
  103.3 1.6 %copy-done.6 = f32[2,512,512]{2,1,0:T(8,128)S(1)} copy-done((f32[2,512,512]{2,1,0:T(8,128)S(1)}, f32[2,512,512]{2,1,0:T(8,128)}, u32[]{:S(2)}) %copy-start.6) | copy-done | bytes 2097176
  104.9 1.6 %copy-done.8 = f32[2,512,512]{2,1,0:T(8,128)S(1)} copy-done((f32[2,512,512]{2,1,0:T(8,128)S(1)}, f32[2,512,512]{2,1,0:T(8,128)}, u32[]{:S(2)}) %copy-start.8) | copy-done | bytes 2097176
  106.4 1.6 %copy-done.10 = f32[1024,512]{1,0:T(8,128)S(1)} copy-done((f32[1024,512]{1,0:T(8,128)S(1)}, f32[1024,512]{1,0:T(8,128)}, u32[]{:S(2)}) %copy-start.10) | copy-done | bytes 2097176
  108.0 10.4 %shard_map.52 = (f32[512,128]{1,0:T(8,128)S(1)}, f32[512,1024]{1,0:T(8,128)S(1)}) custom-call(s32[2,32]{1,0:T(2,128)S(1)} %copy-done.4, f32[2,512,512]{2,1,0:T(8,128)S(1)} %copy-done.6, f32[2,512,512]{2,1,0:T(8,128)S(1)} %copy-done.8, f32[1024,512]{1,0:T(8,128)S(1)} %copy-done.10, f32[512,1536]{1,0:T(8,128)S(1)} %bitcast.24), custom_call_target="tpu_custom_call" | custom-call | flops 8053063680 | bytes 8388608 | tf_op jit(solution)/shard_map/pallas_call | solution.py:497
  118.4 0.0 copy-start
  118.4 1.3 copy-done
  119.7 0.7 copy-done.3
  120.4 0.1 fusion.5
  120.5 0.1 reshape.61
  120.6 0.1 reshape.60
  120.7 0.2 select_reduce_fusion
  120.9 0.1 bitcast_not_fusion.1
  120.9 1.8 %pad_maximum_fusion = f32[2,512,128]{2,1,0:T(8,128)} fusion(f32[1,512,128]{2,1,0:T(8,128)} %bitcast.26, f32[1,512,128]{2,1,0:T(8,128)S(1)} %bitcast.25), kind=kLoop, calls=%fused_computation.9 | loop fusion | flops 131072 | bytes 1048576 | tf_op jit(solution)/shard_map/stack | solution.py:591
  122.7 0.1 compare_bitcast_fusion
  122.8 0.1 bitcast_not_fusion
  122.9 0.1 broadcast_bitcast_fusion.2
  123.0 0.1 broadcast_bitcast_fusion
  123.0 1.5 %and_select_fusion.3 = (f32[512,512]{1,0:T(8,128)S(1)}, f32[512,512]{1,0:T(8,128)S(1)}) fusion(f32[512,512]{1,0:T(8,128)} %get-tuple-element.17, pred[512]{0:T(512)(128)(4,1)S(1)} %bitcast_not_fusion.1, pred[512]{0:T(512)(128)(4,1)S(1)} %get-tuple-element.37, pred[512]{0:T(512)(128)(4,1)S(1)} %get-tuple-element.36), kind=kLoop, calls=%fused_computation.8 | loop fusion | flops 1048576 | bytes 3147264 | tf_op jit(solution)/shard_map/jit(_where)/select_n | solution.py:28
  124.5 0.0 copy-start.1
  124.6 1.6 %collective-permute-done = f32[512,512]{1,0:T(8,128)} collective-permute-done((f32[512,512]{1,0:T(8,128)}, f32[512,512]{1,0:T(8,128)}, u32[]{:S(2)}, u32[]{:S(2)}) %collective-permute-start) | collective-permute-done | bytes 1048608 | tf_op jit(solution)/shard_map/ppermute | solution.py:16
  126.2 1.5 %and_select_fusion.1 = (f32[512,512]{1,0:T(8,128)S(1)}, f32[512,512]{1,0:T(8,128)S(1)}) fusion(f32[512,512]{1,0:T(8,128)} %collective-permute-done, pred[512]{0:T(512)(128)(4,1)S(1)} %bitcast_not_fusion, pred[512]{0:T(512)(128)(4,1)S(1)} %get-tuple-element.39, pred[512]{0:T(512)(128)(4,1)S(1)} %get-tuple-element.38), kind=kLoop, calls=%fused_computation.6 | loop fusion | flops 1048576 | bytes 3147264 | tf_op jit(solution)/shard_map/jit(_where)/select_n | solution.py:28
  127.7 0.7 fusion.2
  128.5 3.5 %copy.7 = f32[512,1,1024]{2,1,0:T(1,128)} copy(f32[512,1,1024]{2,0,1:T(8,128)S(1)} %fusion.2) | data formatting | bytes 4194304
  (21 shorter events, 0.1 us)
Async XLA Ops:
  0.6 2.1 %copy-start.4 = (s32[2,32]{1,0:T(2,128)S(1)}, s32[2,32]{1,0:T(2,128)}, u32[]{:S(2)}) copy-start(s32[2,32]{1,0:T(2,128)} %refs_0_.3) | copy-start | bytes 772
  4.1 1.0 copy-start.2
  95.1 6.8 %copy-start.5 = (f32[2,512,512]{2,1,0:T(8,128)}, f32[2,512,512]{2,1,0:T(8,128)S(1)}, u32[]{:S(2)}) copy-start(f32[2,512,512]{2,1,0:T(8,128)S(1)} %get-tuple-element.10.refs_1_) | copy-start | bytes 6291460
  95.1 6.8 %copy-start.7 = (f32[2,512,512]{2,1,0:T(8,128)}, f32[2,512,512]{2,1,0:T(8,128)S(1)}, u32[]{:S(2)}) copy-start(f32[2,512,512]{2,1,0:T(8,128)S(1)} %get-tuple-element.11.refs_2_) | copy-start | bytes 6291460
  95.1 6.8 %copy-start.9 = (f32[1024,512]{1,0:T(8,128)}, f32[1024,512]{1,0:T(8,128)S(1)}, u32[]{:S(2)}) copy-start(f32[1024,512]{1,0:T(8,128)S(1)} %get-tuple-element.14.refs_3_) | copy-start | bytes 6291460
  101.9 24.3 %collective-permute-start = (f32[512,512]{1,0:T(8,128)}, f32[512,512]{1,0:T(8,128)}, u32[]{:S(2)}, u32[]{:S(2)}) collective-permute-start(f32[512,512]{1,0:T(8,128)} %get-tuple-element.17), channel_id=1, source_target_pairs={{0,16},{16,0},{1,17},{17,1},{2,18},{18,2},{3,19},{19,3},{4,20},{20... | collective-permute-start | bytes 3145736 | tf_op jit(solution)/shard_map/ppermute | solution.py:16
  103.3 1.6 %copy-start.6 = (f32[2,512,512]{2,1,0:T(8,128)S(1)}, f32[2,512,512]{2,1,0:T(8,128)}, u32[]{:S(2)}) copy-start(f32[2,512,512]{2,1,0:T(8,128)} %copy-done.5) | copy-start | bytes 6291460
  104.9 1.6 %copy-start.8 = (f32[2,512,512]{2,1,0:T(8,128)S(1)}, f32[2,512,512]{2,1,0:T(8,128)}, u32[]{:S(2)}) copy-start(f32[2,512,512]{2,1,0:T(8,128)} %copy-done.7) | copy-start | bytes 6291460
  106.4 1.6 %copy-start.10 = (f32[1024,512]{1,0:T(8,128)S(1)}, f32[1024,512]{1,0:T(8,128)}, u32[]{:S(2)}) copy-start(f32[1024,512]{1,0:T(8,128)} %copy-done.9) | copy-start | bytes 6291460
  108.0 12.4 %copy-start.11 = (s32[1,32]{1,0:T(1,128)S(1)}, s32[1,32]{1,0:T(1,128)}, u32[]{:S(2)}) copy-start(s32[1,32]{1,0:T(1,128)} %param.5) | copy-start | bytes 388
  118.4 1.3 %copy-start = (f32[512,1024]{1,0:T(8,128)}, f32[512,1024]{1,0:T(8,128)S(1)}, u32[]{:S(2)}) copy-start(f32[512,1024]{1,0:T(8,128)S(1)} %get-tuple-element.16) | copy-start | bytes 6291460
  119.7 0.7 copy-start.3
  124.5 3.2 %copy-start.1 = (f32[512,1024]{1,0:T(8,128)S(1)}, f32[512,1024]{1,0:T(8,128)}, u32[]{:S(2)}) copy-start(f32[512,1024]{1,0:T(8,128)} %copy-done) | copy-start | bytes 6291460

commit v4 on v3

--- a/solution.py
+++ b/solution.py
@@ -375,12 +375,12 @@
                 own_cols_copy(k).start()
                 for dl, dr in others[k]:
                     col_copy(k, dl, dr).start()
-            for k in range(levels):
-                for slot in range(1, n_col):
-                    for step in range(1, n_col):
-                        row_copy(k, step, slot).start()
 
     advance(0)
+    for k in range(levels):
+        for slot in range(1, n_col):
+            for step in range(1, n_col):
+                row_copy(k, step, slot).start()
     eliminate(inv_ref, levels, pivots, tile, block_row, between)
 
     for k in range(levels):

time: 132 us -> 141 us (1.068)
  Pallas kernels: 107 us -> 116 us
    pallas_call x1, Pallas kernels: 90 us -> 98.9 us  [gather_and_invert(): pl.pallas_call(lambda *refs: gather_kernel(sizes, *refs), out_shape=[squa...]
  transfers between devices with their start and end apart: 1 -> 1, of which waited for: 1 -> 1; matrix products, arithmetic and copies ran while one was open for 3% -> 3% of each run, Pallas kernels for 8% -> 7%
where the time goes in v4:
time: 141 us
  Pallas kernels  116 us (82%)
  local copies, waits for them, and re-layouts  15.1 us (11%)
  other arithmetic  5.94 us (4%)
  waiting for transfers between devices  2.36 us (2%)
    pallas_call x1, Pallas kernels, gather_and_invert(): pl.pallas_call(lambda *refs: gather_kernel(sizes, *refs), out_shape=[squa...  98.9 us
    pallas_call x2, Pallas kernels, panel_and_schur(): pl.pallas_call(lambda *refs: schur_kernel(k, sizes, *refs), grid=(group,)...  17.1 us
    unnamed x26, local copies, waits for them, and re-layouts  13.4 us
    select_n x2, other arithmetic, place_update(): lower_part = jnp.where(row_keep[:, None] & ~col_high[None, :], update, 0.0)  3.01 us
  transfers between devices with their start and end apart: 1, of which 1 were waited for; matrix products, arithmetic and copies ran while one was open for 3% of the time, Pallas kernels for 7%

profile of v4, /device:TPU:0, one launch (start us, length us, event | category | flops | bytes accessed | tf_op | source)
XLA Modules:
  0.0 140.9 jit_solution(1832324871662545671)
XLA Ops:
  0.7 2.1 %copy.10 = f32[512,1,1536]{2,0,1:T(8,128)S(1)} copy(f32[512,1,1536]{2,1,0:T(1,128)} %param.3) | data formatting | bytes 6291456
  2.8 0.1 constant_dynamic-slice_fusion.4
  2.9 0.1 broadcast_in_dim.56
  3.0 1.1 broadcast_in_dim_reshape.22.refs_1_
  4.1 1.0 copy-done.2
  5.1 98.9 %shard_map.50 = (f32[2,512,512]{2,1,0:T(8,128)S(1)}, f32[2,512,512]{2,1,0:T(8,128)S(1)}, f32[512,512]{1,0:T(8,128)S(1)}, f32[1024,512]{1,0:T(8,128)S(1)}) custom-call(f32[512,1536]{1,0:T(8,128)S(1)} %bitcast.22, s32[2,512,1]{2,1,0:T(8,128)S(1)} %copy-done.2, s32[2,1,512]{2,1,0:T(1,128)S(1)} %bitcast.27), custom_call_target="tpu_custom_call" | custom-call | flops 60000002048 | bytes 4194304 | tf_op jit(solution)/shard_map/pallas_call | solution.py:418
  104.1 0.0 copy-start.5
  104.1 6.8 %shard_map.51 = (f32[512,128]{1,0:T(8,128)S(1)}, f32[512,512]{1,0:T(8,128)}) custom-call(s32[2,32]{1,0:T(2,128)S(1)} %copy-done.4, f32[2,512,512]{2,1,0:T(8,128)S(1)} %get-tuple-element.10.refs_1_, f32[2,512,512]{2,1,0:T(8,128)S(1)} %get-tuple-element.11.refs_2_, f32[512,512]{1,0:T(8,128)S(1)} %get-tuple-element.12.refs_3_, f32[512,1536]{1,0:T(8,128)S(1)} %bitcast.23), custom_call_target="tpu_custom_call" | custom-call | flops 4831838208 | bytes 5242880 | tf_op jit(solution)/shard_map/pallas_call | solution.py:497
  110.9 0.6 collective-permute-start
  111.5 1.6 %copy-done.6 = f32[2,512,512]{2,1,0:T(8,128)S(1)} copy-done((f32[2,512,512]{2,1,0:T(8,128)S(1)}, f32[2,512,512]{2,1,0:T(8,128)}, u32[]{:S(2)}) %copy-start.6) | copy-done | bytes 2097176
  113.1 1.6 %copy-done.8 = f32[2,512,512]{2,1,0:T(8,128)S(1)} copy-done((f32[2,512,512]{2,1,0:T(8,128)S(1)}, f32[2,512,512]{2,1,0:T(8,128)}, u32[]{:S(2)}) %copy-start.8) | copy-done | bytes 2097176
  114.7 1.6 %copy-done.10 = f32[1024,512]{1,0:T(8,128)S(1)} copy-done((f32[1024,512]{1,0:T(8,128)S(1)}, f32[1024,512]{1,0:T(8,128)}, u32[]{:S(2)}) %copy-start.10) | copy-done | bytes 2097176
  116.3 10.4 %shard_map.52 = (f32[512,128]{1,0:T(8,128)S(1)}, f32[512,1024]{1,0:T(8,128)S(1)}) custom-call(s32[2,32]{1,0:T(2,128)S(1)} %copy-done.4, f32[2,512,512]{2,1,0:T(8,128)S(1)} %copy-done.6, f32[2,512,512]{2,1,0:T(8,128)S(1)} %copy-done.8, f32[1024,512]{1,0:T(8,128)S(1)} %copy-done.10, f32[512,1536]{1,0:T(8,128)S(1)} %bitcast.24), custom_call_target="tpu_custom_call" | custom-call | flops 8053063680 | bytes 8388608 | tf_op jit(solution)/shard_map/pallas_call | solution.py:497
  126.6 0.0 copy-start
  126.7 1.3 copy-done
  128.0 0.7 copy-done.3
  128.7 0.1 fusion.5
  128.8 0.1 reshape.61
  128.8 0.1 reshape.60
  128.9 0.2 select_reduce_fusion
  129.1 0.1 bitcast_not_fusion.1
  129.2 1.8 %pad_maximum_fusion = f32[2,512,128]{2,1,0:T(8,128)} fusion(f32[1,512,128]{2,1,0:T(8,128)} %bitcast.26, f32[1,512,128]{2,1,0:T(8,128)S(1)} %bitcast.25), kind=kLoop, calls=%fused_computation.9 | loop fusion | flops 131072 | bytes 1048576 | tf_op jit(solution)/shard_map/stack | solution.py:591
  131.0 0.1 compare_bitcast_fusion
  131.0 0.1 bitcast_not_fusion
  131.1 0.1 broadcast_bitcast_fusion.2
  131.2 0.1 broadcast_bitcast_fusion
  131.3 1.5 %and_select_fusion.3 = (f32[512,512]{1,0:T(8,128)S(1)}, f32[512,512]{1,0:T(8,128)S(1)}) fusion(f32[512,512]{1,0:T(8,128)} %get-tuple-element.17, pred[512]{0:T(512)(128)(4,1)S(1)} %bitcast_not_fusion.1, pred[512]{0:T(512)(128)(4,1)S(1)} %get-tuple-element.37, pred[512]{0:T(512)(128)(4,1)S(1)} %get-tuple-element.36), kind=kLoop, calls=%fused_computation.8 | loop fusion | flops 1048576 | bytes 3147264 | tf_op jit(solution)/shard_map/jit(_where)/select_n | solution.py:28
  132.8 0.0 copy-start.1
  132.8 2.4 %collective-permute-done = f32[512,512]{1,0:T(8,128)} collective-permute-done((f32[512,512]{1,0:T(8,128)}, f32[512,512]{1,0:T(8,128)}, u32[]{:S(2)}, u32[]{:S(2)}) %collective-permute-start) | collective-permute-done | bytes 1048608 | tf_op jit(solution)/shard_map/ppermute | solution.py:16
  135.1 1.5 %and_select_fusion.1 = (f32[512,512]{1,0:T(8,128)S(1)}, f32[512,512]{1,0:T(8,128)S(1)}) fusion(f32[512,512]{1,0:T(8,128)} %collective-permute-done, pred[512]{0:T(512)(128)(4,1)S(1)} %bitcast_not_fusion, pred[512]{0:T(512)(128)(4,1)S(1)} %get-tuple-element.39, pred[512]{0:T(512)(128)(4,1)S(1)} %get-tuple-element.38), kind=kLoop, calls=%fused_computation.6 | loop fusion | flops 1048576 | bytes 3147264 | tf_op jit(solution)/shard_map/jit(_where)/select_n | solution.py:28
  136.7 0.7 fusion.2
  137.4 3.5 %copy.7 = f32[512,1,1024]{2,1,0:T(1,128)} copy(f32[512,1,1024]{2,0,1:T(8,128)S(1)} %fusion.2) | data formatting | bytes 4194304
  (21 shorter events, 0.1 us)
Async XLA Ops:
  0.6 2.1 %copy-start.4 = (s32[2,32]{1,0:T(2,128)S(1)}, s32[2,32]{1,0:T(2,128)}, u32[]{:S(2)}) copy-start(s32[2,32]{1,0:T(2,128)} %refs_0_.3) | copy-start | bytes 772
  4.1 1.0 copy-start.2
  104.1 6.8 %copy-start.5 = (f32[2,512,512]{2,1,0:T(8,128)}, f32[2,512,512]{2,1,0:T(8,128)S(1)}, u32[]{:S(2)}) copy-start(f32[2,512,512]{2,1,0:T(8,128)S(1)} %get-tuple-element.10.refs_1_) | copy-start | bytes 6291460
  104.1 6.8 %copy-start.7 = (f32[2,512,512]{2,1,0:T(8,128)}, f32[2,512,512]{2,1,0:T(8,128)S(1)}, u32[]{:S(2)}) copy-start(f32[2,512,512]{2,1,0:T(8,128)S(1)} %get-tuple-element.11.refs_2_) | copy-start | bytes 6291460
  104.1 6.8 %copy-start.9 = (f32[1024,512]{1,0:T(8,128)}, f32[1024,512]{1,0:T(8,128)S(1)}, u32[]{:S(2)}) copy-start(f32[1024,512]{1,0:T(8,128)S(1)} %get-tuple-element.14.refs_3_) | copy-start | bytes 6291460
  110.9 24.2 %collective-permute-start = (f32[512,512]{1,0:T(8,128)}, f32[512,512]{1,0:T(8,128)}, u32[]{:S(2)}, u32[]{:S(2)}) collective-permute-start(f32[512,512]{1,0:T(8,128)} %get-tuple-element.17), channel_id=1, source_target_pairs={{0,16},{16,0},{1,17},{17,1},{2,18},{18,2},{3,19},{19,3},{4,20},{20... | collective-permute-start | bytes 3145736 | tf_op jit(solution)/shard_map/ppermute | solution.py:16
  111.5 1.6 %copy-start.6 = (f32[2,512,512]{2,1,0:T(8,128)S(1)}, f32[2,512,512]{2,1,0:T(8,128)}, u32[]{:S(2)}) copy-start(f32[2,512,512]{2,1,0:T(8,128)} %copy-done.5) | copy-start | bytes 6291460
  113.1 1.6 %copy-start.8 = (f32[2,512,512]{2,1,0:T(8,128)S(1)}, f32[2,512,512]{2,1,0:T(8,128)}, u32[]{:S(2)}) copy-start(f32[2,512,512]{2,1,0:T(8,128)} %copy-done.7) | copy-start | bytes 6291460
  114.7 1.6 %copy-start.10 = (f32[1024,512]{1,0:T(8,128)S(1)}, f32[1024,512]{1,0:T(8,128)}, u32[]{:S(2)}) copy-start(f32[1024,512]{1,0:T(8,128)} %copy-done.9) | copy-start | bytes 6291460
  116.3 12.4 %copy-start.11 = (s32[1,32]{1,0:T(1,128)S(1)}, s32[1,32]{1,0:T(1,128)}, u32[]{:S(2)}) copy-start(s32[1,32]{1,0:T(1,128)} %param.5) | copy-start | bytes 388
  126.6 1.3 copy-start
  128.0 0.7 copy-start.3
  132.8 3.9 %copy-start.1 = (f32[512,1024]{1,0:T(8,128)S(1)}, f32[512,1024]{1,0:T(8,128)}, u32[]{:S(2)}) copy-start(f32[512,1024]{1,0:T(8,128)} %copy-done) | copy-start | bytes 6291460
